TPU v7x, 32 devices: a whole 2x2x4 slice. The times are simulated.
32 devices in a mesh: group: 8 (over y, x, core), pos: 4 (over z).
Axes of the slice: x: 2, y: 2, z: 4, core: 2. Of those that a mesh axis runs over, the one named last changes fastest.
Arguments:
- potential: float32 [4, 2, 1536, 512], P(None, None, 'group', 'pos'), may hold values from -0.3 to 0.3
- probe: float32 [8, 4, 128, 256], P('group', None, 'pos'), may hold values from -3 to 3
- amplitudes: bfloat16 [8, 4, 3, 128, 128], P('group', 'pos'), may hold values from 0.1 to 8, as said below
- row_offset: int32 [8, 4, 3], P('group', 'pos'), may hold values from 0 to 64
- col_offset: int32 [8, 4, 3], P('group', 'pos'), may hold values from 0 to 127
- counts: int32 [8, 4], P('group', 'pos'), may hold values from 1 to 3, as said below
Outputs:
- object_grad: float32 [4, 2, 1536, 512], P(None, None, 'group', 'pos')
- probe_grad: float32 [8, 4, 128, 256], P('group', None, 'pos')
Inputs may be any that keep to these rules, and one draw needn't show every extreme that they name: A tile's positions fill its first counts slots and later slots are unused; at least one tile has 3. `amplitudes`: every entry is positive.
All inputs are finite; a program needn't handle non-finite values.
Results may differ from a plain program's by a relative error of at most 0.02.
The roundings to bfloat16 on the way count: a program that leaves them out, or rounds other values in their place, can miss the bound.
Values sent between devices are 32-bit elements; how exact they have to be, the bound alone decides.
No kernel may reach another device: no remote copies, remote signals or barrier semaphores. Data moves between devices by JAX's collectives and lax.ppermute only.
A program may use at most 64 MiB of HBM per device.

v0:
```python
import functools
import math

import jax
import jax.numpy as jnp
import ml_dtypes
import numpy as np
from jax import lax
from jax.experimental import pallas as pl
from jax.experimental.pallas import tpu as pltpu
from jax.sharding import PartitionSpec as P

PROP = 0.25
REG = 0.1
VMEM = pl.BlockSpec(memory_space=pltpu.VMEM)
SMEM = pl.BlockSpec(memory_space=pltpu.SMEM)


@functools.lru_cache(maxsize=None)
def tables(size):
    idx = np.arange(size)
    angle = np.float32(2.0 * math.pi / size) * (idx[:, None] * idx[None, :] % size).astype(np.float32)
    cosv = (np.cos(angle) / np.float32(math.sqrt(size))).astype(ml_dtypes.bfloat16).astype(np.float64)
    sinv = (np.sin(angle) / np.float32(math.sqrt(size))).astype(ml_dtypes.bfloat16).astype(np.float64)
    forward = np.block([[cosv, -sinv], [sinv, cosv]])
    inverse = np.block([[cosv, sinv], [-sinv, cosv]])
    freq = np.where(idx < size // 2, idx, idx - size).astype(np.float64)
    phase = -2.0 * math.pi * PROP / size * freq * freq
    real, imag = np.diag(np.cos(phase)), np.diag(np.sin(phase))
    ahead = forward @ np.block([[real, imag], [-imag, real]]) @ inverse
    behind = forward @ np.block([[real, -imag], [imag, real]]) @ inverse
    rows = np.arange(2 * size).reshape(2, size // 8, 8).swapaxes(0, 1).reshape(-1)
    left = [t.T[rows] for t in (forward, inverse, ahead, behind)]
    return np.stack([forward, inverse, ahead, behind, *left]).astype(ml_dtypes.bfloat16)


def mul(a, b):
    return a[0] * b[0] - a[1] * b[1], a[0] * b[1] + a[1] * b[0]


def mulc(a, b):
    return a[0] * b[0] + a[1] * b[1], a[0] * b[1] - a[1] * b[0]


def sine(x):
    y = x * x
    return x * (1.0 - y * (1 / 6) * (1.0 - y * (1 / 20) * (1.0 - y * (1 / 42) * (1.0 - y * (1 / 72)))))


def cosine(x):
    y = x * x
    return 1.0 - y * 0.5 * (1.0 - y * (1 / 12) * (1.0 - y * (1 / 30) * (1.0 - y * (1 / 56) * (1.0 - y * (1 / 90)))))


def transform(waves, right, left):
    size = waves[0][0].shape[0]
    pairs = [waves[first : first + 2] for first in range(0, len(waves), 2)]
    mids = []
    for pair in pairs:
        rows = jnp.concatenate(
            [jnp.concatenate([re.astype(jnp.bfloat16), im.astype(jnp.bfloat16)], 1) for re, im in pair], 0
        )
        mid = jnp.dot(rows, right, preferred_element_type=jnp.float32).astype(jnp.bfloat16)
        cut = [mid[i * size : (i + 1) * size] for i in range(len(pair))]
        mids.append(jnp.concatenate([jnp.concatenate([m[:, :size], m[:, size:]], 0) for m in cut], 1))
    out = []
    for pair, mid in zip(pairs, mids):
        done = jnp.dot(left, mid, preferred_element_type=jnp.float32)
        done = done.reshape(size // 8, 2, 8, -1)
        parts = [done[:, c].reshape(size, -1) for c in range(2)]
        for i in range(len(pair)):
            out.append(tuple(x[:, i * size : (i + 1) * size] for x in parts))
    return out


def swap(values, half):
    return pltpu.roll(values, half, values.ndim - 1)


def low_lanes(shape):
    return lax.broadcasted_iota(jnp.int32, shape, len(shape) - 1) < shape[-1] // 2


def pack(pair):
    half = pair[0].shape[-1] // 2
    low = low_lanes(pair[0].shape)
    return jnp.where(low, pair[0], swap(pair[1], half)), jnp.where(low, swap(pair[0], half), pair[1])


def unpack(lows, highs):
    half = lows.shape[-1] // 2
    low = low_lanes(lows.shape)
    return jnp.where(low, lows, swap(highs, half)), jnp.where(low, swap(lows, half), highs)


def pack_kernel(groups, me_ref, row_ref, col_ref, count_ref, potential_ref, amps_ref, *refs):
    slots = row_ref.shape[0]
    even = lax.rem(me_ref[0], 2) == 0
    _, _, rows, size = potential_ref.shape
    for g, group in enumerate(groups):
        first, second = refs[2 * g : 2 * g + 2]
        for j, s in enumerate(group):
            lows, highs = pack((potential_ref[s, 0], potential_ref[s, 1]))
            first[j * rows : (j + 1) * rows] = jnp.where(even, highs, lows)
            second[j * rows : (j + 1) * rows] = jnp.where(even, lows, highs)
        top = len(group) * rows
        if g == 0:
            lane = lax.broadcasted_iota(jnp.int32, (8, size), 1)
            about = jnp.zeros((8, size), jnp.int32)
            for p in range(slots):
                about = jnp.where(lane == p, row_ref[p], jnp.where(lane == slots + p, col_ref[p], about))
            about = jnp.where(lane == 2 * slots, count_ref[0], about).astype(jnp.float32)
            first[top:] = about
            second[top:] = about
        else:
            for p in range(slots):
                amps = amps_ref[p].astype(jnp.float32)
                first[top + p * size : top + (p + 1) * size] = amps
                second[top + p * size : top + (p + 1) * size] = amps


def transmit(phase, absorption):
    magnitude = jnp.exp(-absorption)
    return magnitude * cosine(phase), magnitude * sine(phase)


def gate_kernel(*refs):
    pass


def prepare_kernel(potential_ref, tables_ref, amps_ref, pieces_ref, trans_ref, tables_out, amps_out, probe_ref):
    part = pieces_ref.shape[2]
    for k in range(pieces_ref.shape[0]):
        probe_ref[:, k * part : (k + 1) * part, :] = pieces_ref[k]
    for s in range(potential_ref.shape[0]):
        trans_ref[s, 0], trans_ref[s, 1] = transmit(potential_ref[s, 0], potential_ref[s, 1])
    tables_out[...] = tables_ref[...]
    amps_out[...] = amps_ref[...]


class Names:
    def __init__(self, names, refs):
        self.__dict__.update(zip(names, refs))

    def get(self, name):
        return self.__dict__[name]


def stage_kernel(names, ahead, top, back, pieces, *refs):
    r = Names(names, refs)
    size = r.tables.shape[-1] // 2
    half = size // 2
    modes = r.modes_ref.shape[0]
    slots = r.rows.shape[0]
    me = r.me[0]
    last = me == pieces - 1
    even = lax.rem(me, 2) == 0
    lanes = lax.broadcasted_iota(jnp.int32, (size, size), 1)

    def halves(i, start, count):
        one, two = r.across_even[start : start + count], r.across_odd[start : start + count]
        return jnp.where(even, one, two), jnp.where(even, two, one)

    if 0 in ahead:
        height = r.own.shape[-2]
        about = halves(0, len(ahead) * height, 8)[1][0:1].astype(jnp.int32)
        lane = lanes[0:1]
        number = jnp.int32(0)
        for k in range(2 * slots):
            p = k % slots
            if k < slots:
                row, col, count = r.rows[p], r.cols[p], r.count[0]
                stays = (col < half) | last
            else:
                row, col, count = [jnp.sum(jnp.where(lane == at, about, 0)) for at in (p, slots + p, 2 * slots)]
                stays = col >= half
            r.held_out[3 * number + 1] = jnp.int32(k)
            r.held_out[3 * number + 2] = row
            r.held_out[3 * number + 3] = col
            number = number + ((p < count) & stays).astype(jnp.int32)
        r.held_out[0] = number
        held = r.held_out
    else:
        held = r.held
    number = held[0]

    for i, s in enumerate(ahead):
        height = r.own.shape[-2]
        halo = transmit(*unpack(*halves(0, i * height, height)))
        for c in range(2):
            r.tiles[i, 0, c] = r.own[s, c]
            r.tiles[i, 1, c] = halo[c]
            r.tiles[i, 2, c] = jnp.full((height, size), 1.0 - c, jnp.float32)
    if top:
        begin = len(ahead) * r.own.shape[-2]
        for p in range(slots):
            r.amps_all[p] = r.amps[p].astype(jnp.float32)
            r.amps_all[slots + p] = halves(0, begin + p * size, size)[1]
    if back:
        r.grads[...] = jnp.zeros_like(r.grads)
    if 0 in back:
        r.total[...] = jnp.zeros_like(r.total)

    def load(ref, *lead):
        return [(ref[(*lead, m, slice(None), slice(0, size))], ref[(*lead, m, slice(None), slice(size, None))]) for m in range(modes)]

    def store(ref, waves, *lead):
        for m, (re, im) in enumerate(waves):
            ref[(*lead, m, slice(None), slice(0, size))] = re
            ref[(*lead, m, slice(None), slice(size, None))] = im

    def psi(s, at):
        return load(r.psi_0) if s == 0 else load(r.get("psi_%d" % s), at)

    def trans(s, at):
        ref = r.get("trans_%d" % s)
        return ref[at, 0], ref[at, 1]

    def slot_step(at, misfit):
        k = held[3 * at + 1]
        row = held[3 * at + 2]
        col = held[3 * at + 3]
        own = k < slots
        left = jnp.where(own, 0, 1)
        right = jnp.where(own, jnp.where(last, 2, 1), 0)
        turn = lax.rem(size - col, size)
        inside = lanes >= col
        for i, s in enumerate(ahead):
            for c in range(2):
                both = jnp.where(inside, r.tiles[i, left, c, pl.ds(row, size), :], r.tiles[i, right, c, pl.ds(row, size), :])
                r.get("trans_%d" % s)[at, c] = pltpu.roll(both, turn, 1)
            waves = [mul(trans(s, at), w) for w in psi(s, at)]
            if top and s == ahead[-1]:
                waves = transform(waves, r.tables[0], r.tables[4])
            else:
                waves = transform(waves, r.tables[2], r.tables[6])
                store(r.get("psi_%d" % (s + 1)), waves, at)
        if top:
            inten = sum(re * re + im * im for re, im in waves)
            model = jnp.sqrt(inten + REG)
            observed = r.amps_all[k]
            diff = model - observed
            misfit = misfit + jnp.sum(diff * diff, axis=0, keepdims=True)
            ratio = 1.0 - observed / model
            waves = transform([(ratio * re, ratio * im) for re, im in waves], r.tables[1], r.tables[5])
        elif back:
            waves = load(r.wave_in, at)
        for i, s in enumerate(back):
            waves = [mulc(trans(s, at), w) for w in waves]
            quot = [mulc(a, w) for a, w in zip(psi(s, at), waves)]
            values = sum(im for _, im in quot), -sum(re for re, _ in quot)
            for c in range(2):
                turned = pltpu.roll(values[c], col, 1)
                r.grads[i, left, c, pl.ds(row, size), :] += jnp.where(inside, turned, 0.0)
                r.grads[i, right, c, pl.ds(row, size), :] += jnp.where(inside, 0.0, turned)
            if s > 0:
                waves = transform(waves, r.tables[3], r.tables[7])
        if 0 in back:
            for m, (re, im) in enumerate(waves):
                r.total[m, :, :size] += re
                r.total[m, :, size:] += im
        elif back or top:
            store(r.wave_out, waves, at)
        return misfit

    misfit = lax.fori_loop(0, number, slot_step, jnp.zeros((1, size), jnp.float32))
    if top:
        value = jnp.sum(misfit, axis=1, keepdims=True)
        lane = lax.broadcasted_iota(jnp.int32, (1, 1, size), 2)
        count = r.count[0].astype(jnp.float32)
        value = jnp.where(lane == 0, value[None], jnp.where(lane == 1, count, 0.0))
        r.sums[...] = jnp.broadcast_to(value[0], r.sums.shape)
    for i, s in enumerate(back):
        r.grad[i] = r.grads[i, 0]
        lows, highs = pack((r.grads[i, 1, 0], r.grads[i, 1, 1]))
        height = lows.shape[0]
        r.for_even[i * height : (i + 1) * height] = jnp.where(even, lows, highs)
        r.for_odd[i * height : (i + 1) * height] = jnp.where(even, highs, lows)
    if 0 in back:
        part = r.total.shape[1] // pieces
        sums = r.sums_in[...]
        for k in range(pieces):
            for m in range(modes):
                r.share[k, m * part : (m + 1) * part] = r.total[m, k * part : (k + 1) * part, :]
            r.share[k, modes * part :] = jnp.concatenate([sums, sums], 1)


def stage(given, made, scratch, ahead, top, back, pieces, name):
    names = [n for n, _, _ in given] + [n for n, _ in made] + [n for n, _ in scratch]
    out = pl.pallas_call(
        functools.partial(stage_kernel, names, ahead, top, back, pieces),
        out_shape=[jax.ShapeDtypeStruct(shape, jnp.float32) for _, shape in made],
        in_specs=[SMEM if small else VMEM for _, _, small in given],
        out_specs=[VMEM] * len(made),
        scratch_shapes=[x for _, x in scratch],
        compiler_params=pltpu.CompilerParams(vmem_limit_bytes=24 * 2**20),
        cost_estimate=pl.CostEstimate(flops=(len(ahead) + len(back) + 1) * 10**9, bytes_accessed=10**7, transcendentals=0),
        name=name,
    )(*[x for _, x, _ in given])
    return dict(zip([n for n, _ in made], out))


def finish_kernel(back, modes, me_ref, late_ref, early_ref, even_in, odd_in, share_in, sums_ref, grad_ref, share_ref):
    even = lax.rem(me_ref[0], 2) == 0
    rows, size = grad_ref.shape[2:]
    part = share_ref.shape[2]
    sums = sums_ref[0:1]
    scale = lax.rsqrt(sums[:, 0:1] / (sums[:, 1:2] * (size * size)) + 1e-06)
    for i, s in enumerate(back):
        one, two = even_in[i * rows : (i + 1) * rows], odd_in[i * rows : (i + 1) * rows]
        arrived = unpack(jnp.where(even, two, one), jnp.where(even, one, two))
        count = late_ref.shape[0]
        for c in range(2):
            own = late_ref[i, c] if i < count else early_ref[i - count, c]
            grad_ref[s, c] = (own + arrived[c]) * scale
    for m in range(modes):
        share_ref[0, m] = jnp.sum(share_in[:, m * part : (m + 1) * part, :], axis=0) * scale


def total_over(value, axis):
    n = lax.axis_size(axis)
    if n & (n - 1):
        return lax.psum(value, axis)
    step = 1
    while step < n:
        ways = 4 if n // step % 4 == 0 else 2
        value = value + sum(
            lax.ppermute(value, axis, [(i, i ^ (step * k)) for i in range(n)]) for k in range(1, ways)
        )
        step *= ways
    return value


def body(potential, probe, amplitudes, row_offset, col_offset, counts):
    slices, _, rows, size = potential.shape
    modes = probe.shape[1]
    part = probe.shape[2]
    slots = row_offset.shape[-1]
    pieces = lax.axis_size("pos")
    cut = slices // 2
    groups = (tuple(range(cut)), tuple(range(cut, slices)))
    f32 = jnp.float32
    me = lax.axis_index("pos").astype(jnp.int32).reshape(1)
    here = [row_offset[0, 0], col_offset[0, 0], counts[0]]

    def exchange(value, first):
        edges = [(i, i + 1) for i in range(first, pieces - 1, 2)]
        return lax.ppermute(value, "pos", edges + [(j, i) for i, j in edges])

    def call(kernel, given, out, name, scratch=(), flops=0):
        return pl.pallas_call(
            kernel,
            out_shape=[x[0] if isinstance(x, tuple) else x for x in out],
            in_specs=[SMEM if jnp.issubdtype(x.dtype, jnp.integer) else VMEM for x in given],
            out_specs=[SMEM if jnp.issubdtype(x.dtype, jnp.integer) else VMEM for x in out],
            scratch_shapes=list(scratch),
            compiler_params=pltpu.CompilerParams(vmem_limit_bytes=24 * 2**20),
            cost_estimate=pl.CostEstimate(flops=flops, bytes_accessed=10**6, transcendentals=0),
            name=name,
        )(*given)

    def array(shape, dtype=f32):
        return jax.ShapeDtypeStruct(shape, dtype)

    def stage(given, made, scratch, ahead, top, back, name):
        given = dict(me=me, rows=here[0], cols=here[1], count=here[2], tables=tables_here, **given)
        scratch = dict(modes_ref=pltpu.SMEM((modes,), jnp.int32), **scratch)
        names = list(given) + list(made) + list(scratch)
        kernel = functools.partial(stage_kernel, names, ahead, top, back, pieces)
        flops = (len(ahead) + len(back) + 1) * 2 * 10**9
        return dict(zip(made, call(kernel, list(given.values()), list(made.values()), name, scratch.values(), flops)))

    gathered = lax.all_to_all(jnp.broadcast_to(probe, (pieces,) + probe.shape[1:]), "pos", 0, 0)
    heights = [len(groups[0]) * rows + 8, len(groups[1]) * rows + slots * size]
    packed = call(
        functools.partial(pack_kernel, groups),
        [me, *here, potential, amplitudes[0, 0]],
        [array((heights[i // 2], size)) for i in range(4)],
        "pack",
    )
    came = [exchange(packed[i], i % 2) for i in range(4)]
    trans_own, tables_here, amps, probe_all = call(
        prepare_kernel,
        [potential, jnp.asarray(tables(size)), amplitudes[0, 0], gathered],
        [
            array(potential.shape),
            array((8, 2 * size, 2 * size), jnp.bfloat16),
            array((slots, size, size), jnp.bfloat16),
            array((modes, size, 2 * size)),
        ],
        "prepare",
        flops=10**9,
    )

    wave = (2 * slots, modes, size, 2 * size)
    trans = (2 * slots, 2, size, size)
    tiles = lambda n: pltpu.VMEM((n, 3, 2, rows, size), f32)
    sides = lambda n: dict(grad=array((n, 2, rows, size)), for_even=array((n * rows, size)), for_odd=array((n * rows, size)))

    first, second = groups
    a = stage(
        dict(own=trans_own, across_even=came[0], across_odd=came[1], psi_0=probe_all),
        dict(held_out=array((6 * slots + 4,), jnp.int32))
        | {"psi_%d" % (s + 1): array(wave) for s in first}
        | {"trans_%d" % s: array(trans) for s in first},
        dict(tiles=tiles(len(first))),
        first,
        False,
        (),
        "ahead",
    )
    held = a["held_out"]
    b = stage(
        dict(own=trans_own, across_even=came[2], across_odd=came[3], amps=amps, held=held)
        | {"psi_%d" % second[0]: a["psi_%d" % second[0]]},
        dict(sums=array((8, size)), wave_out=array(wave)) | sides(len(second)),
        dict(tiles=tiles(len(second)), grads=tiles(len(second)), amps_all=pltpu.VMEM((2 * slots, size, size), f32))
        | {"psi_%d" % s: pltpu.VMEM(wave, f32) for s in second[1:]}
        | {"trans_%d" % s: pltpu.VMEM(trans, f32) for s in second},
        second,
        True,
        second[::-1],
        "top",
    )
    c = stage(
        dict(held=held, wave_in=b["wave_out"], sums_in=b["sums"])
        | {"psi_%d" % s: probe_all if s == 0 else a["psi_%d" % s] for s in first}
        | {"trans_%d" % s: a["trans_%d" % s] for s in first},
        dict(share=array((pieces, modes * part + 8, 2 * size))) | sides(len(first)),
        dict(grads=tiles(len(first)), total=pltpu.VMEM(wave[1:], f32)),
        (),
        False,
        first[::-1],
        "back",
    )
    join = lambda name: jnp.concatenate([b[name], c[name]], 0)
    got = [exchange(join("for_even"), 0), exchange(join("for_odd"), 1)]
    shares = lax.all_to_all(c["share"], "pos", 0, 0)
    sums = total_over(jnp.sum(shares[:, modes * part :, :size], axis=0), "group")
    return call(
        functools.partial(finish_kernel, second[::-1] + first[::-1], modes),
        [me, b["grad"], c["grad"], *got, shares, sums],
        [array(potential.shape), array(probe.shape)],
        "finish",
    )


def solution(mesh):
    placed = (
        P(None, None, "group", "pos"),
        P("group", None, "pos", None),
        P("group", "pos", None, None, None),
        P("group", "pos", None),
        P("group", "pos", None),
        P("group", "pos"),
    )
    return jax.shard_map(
        body,
        mesh=mesh,
        in_specs=placed,
        out_specs=(P(None, None, "group", "pos"), P("group", None, "pos", None)),
        check_vma=False,
    )
```

profile of v0, /device:TPU:0, one launch (start us, length us, event | category | flops | bytes accessed | tf_op | source)
XLA Modules:
  0.0 75.0 jit_solution(985218849146197824)
XLA Ops:
  0.6 0.0 copy-start.5
  0.6 0.0 copy-start.7
  0.7 1.8 %broadcast_in_dim.8 = f32[4,4,32,256]{3,2,1,0:T(8,128)} broadcast(f32[4,32,256]{2,1,0:T(8,128)} %bitcast.20), dimensions={1,2,3} | broadcast | bytes 655360 | tf_op jit(solution)/shard_map/broadcast_in_dim | solution.py:373
  2.4 6.3 %all-to-all-start = ((f32[4,4,32,256]{3,2,1,0:T(8,128)}), f32[4,4,32,256]{3,2,1,0:T(8,128)S(1)}, u32[]{:S(2)}, u32[]{:S(2)}) async-start(f32[4,4,32,256]{3,2,1,0:T(8,128)} %broadcast_in_dim.8), calls=%async_computation | async-start | bytes 1048576 | tf_op jit(solution)/shard_map/all_to_all | solution.py:373
  9.4 0.0 copy-start
  9.4 1.1 %copy-done = f32[4,2,192,128]{3,2,1,0:T(8,128)S(1)} copy-done((f32[4,2,192,128]{3,2,1,0:T(8,128)S(1)}, f32[4,2,192,128]{3,2,1,0:T(8,128)}, u32[]{:S(2)}) %copy-start) | copy-done | bytes 786456
  10.5 0.0 copy-start.2
  10.5 0.9 %copy-done.2 = bf16[1,1,3,128,128]{4,3,2,1,0:T(8,128)(2,1)S(1)} copy-done((bf16[1,1,3,128,128]{4,3,2,1,0:T(8,128)(2,1)S(1)}, bf16[1,1,3,128,128]{4,3,2,1,0:T(8,128)(2,1)}, u32[]{:S(2)}) %copy-start.2) | copy-done | bytes 98328
  11.4 0.0 copy-start.4
  11.4 0.7 copy-done.4
  12.1 0.0 copy-start.6
  12.1 0.7 copy-done.6
  12.7 0.8 %pack.1 = (f32[392,128]{1,0:T(8,128)S(1)}, f32[392,128]{1,0:T(8,128)S(1)}, f32[768,128]{1,0:T(8,128)S(1)}, f32[768,128]{1,0:T(8,128)S(1)}) custom-call(s32[1]{0:T(128)} %bitcast.me_ref.refs_0_, s32[3]{0:T(128)S(1)} %bitcast.12, s32[3]{0:T(128)S(1)} %bitcast.16, s32[1]{0:T(128)} %bitcast.6.count_ref, f32[4,2,192,128]{3,2,1,0:T(8,128)S(1)} %copy-done, ...), custom_call_target="tpu_custom_call" | custom-call | bytes 1000000 | tf_op jit(solution)/shard_map/pack/pallas_call | solution.py:351
  13.6 2.1 %collective-permute-start.2 = (f32[392,128]{1,0:T(8,128)S(1)}, f32[392,128]{1,0:T(8,128)S(1)}, u32[]{:S(2)}, u32[]{:S(2)}) collective-permute-start(f32[392,128]{1,0:T(8,128)S(1)} %get-tuple-element.29), channel_id=1, source_target_pairs={{0,1},{2,3},{1,0},{3,2},{4,5},{6,7},{5,4},{7,6},{8,9},{10,11},{9,8... | collective-permute-start | bytes 602120 | tf_op jit(solution)/shard_map/ppermute | solution.py:348
  15.6 0.7 collective-permute-start.3
  16.3 4.2 %collective-permute-start = (f32[768,128]{1,0:T(8,128)S(1)}, f32[768,128]{1,0:T(8,128)S(1)}, u32[]{:S(2)}, u32[]{:S(2)}) collective-permute-start(f32[768,128]{1,0:T(8,128)S(1)} %get-tuple-element.26), channel_id=1, source_target_pairs={{0,1},{2,3},{1,0},{3,2},{4,5},{6,7},{5,4},{7,6},{8,9},{10,11},{9,8... | collective-permute-start | bytes 1179656 | tf_op jit(solution)/shard_map/ppermute | solution.py:348
  20.5 0.7 collective-permute-start.1
  21.2 3.0 %all-to-all-done.pieces_ref = f32[4,4,32,256]{3,2,1,0:T(8,128)S(1)} async-done(((f32[4,4,32,256]{3,2,1,0:T(8,128)}), f32[4,4,32,256]{3,2,1,0:T(8,128)S(1)}, u32[]{:S(2)}, u32[]{:S(2)}) %all-to-all-start) | async-done | bytes 524320 | tf_op jit(solution)/shard_map/all_to_all | solution.py:373
  24.3 0.0 copy-start.1
  24.3 1.1 %copy-done.1 = f32[4,2,192,128]{3,2,1,0:T(8,128)S(1)} copy-done((f32[4,2,192,128]{3,2,1,0:T(8,128)S(1)}, f32[4,2,192,128]{3,2,1,0:T(8,128)}, u32[]{:S(2)}) %copy-start.1) | copy-done | bytes 786456
  25.4 0.0 copy-start.3
  25.4 0.9 %copy-done.3 = bf16[1,1,3,128,128]{4,3,2,1,0:T(8,128)(2,1)S(1)} copy-done((bf16[1,1,3,128,128]{4,3,2,1,0:T(8,128)(2,1)S(1)}, bf16[1,1,3,128,128]{4,3,2,1,0:T(8,128)(2,1)}, u32[]{:S(2)}) %copy-start.3) | copy-done | bytes 98328
  26.3 0.0 copy-start.8
  26.3 1.2 %copy-done.8 = bf16[8,256,256]{2,1,0:T(8,128)(2,1)S(1)} copy-done((bf16[8,256,256]{2,1,0:T(8,128)(2,1)S(1)}, bf16[8,256,256]{2,1,0:T(8,128)(2,1)}, u32[]{:S(2)}) %copy-start.8) | copy-done | bytes 1048600
  27.5 0.5 prepare.1
  28.0 0.0 collective-permute-done.2.refs_6_
  28.0 0.0 collective-permute-done.3.refs_7_
  28.0 0.0 copy-done.5
  28.0 0.0 copy-done.7
  28.0 2.4 %ahead.1 = (s32[22]{0:T(128)S(1)}, f32[6,4,128,256]{3,2,1,0:T(8,128)S(1)}, f32[6,4,128,256]{3,2,1,0:T(8,128)S(1)}, f32[6,2,128,128]{3,2,1,0:T(8,128)S(1)}, f32[6,2,128,128]{3,2,1,0:T(8,128)S(1)}) custom-call(s32[1]{0:T(128)} %bitcast.me_ref.refs_0_, s32[3]{0:T(128)S(1)} %bitcast.13, s32[3]{0:T(128)S(1)} %bitcast.17, s32[1]{0:T(128)} %bitcast.7.refs_3_, ...), custom_call_target="tpu_custom_call" | custom-call | flops 6000000000 | bytes 1000000 | tf_op jit(solution)/shard_map/ahead/pallas_call | solution.py:351
  30.5 1.8 %collective-permute-done.refs_6_ = f32[768,128]{1,0:T(8,128)S(1)} collective-permute-done((f32[768,128]{1,0:T(8,128)S(1)}, f32[768,128]{1,0:T(8,128)S(1)}, u32[]{:S(2)}, u32[]{:S(2)}) %collective-permute-start) | collective-permute-done | bytes 393248 | tf_op jit(solution)/shard_map/ppermute | solution.py:348
  32.2 0.0 collective-permute-done.1.refs_7_
  32.3 3.3 %top.1 = (f32[8,128]{1,0:T(8,128)S(1)}, f32[6,4,128,256]{3,2,1,0:T(8,128)S(1)}, f32[2,2,192,128]{3,2,1,0:T(8,128)S(1)}, f32[384,128]{1,0:T(8,128)S(1)}, f32[384,128]{1,0:T(8,128)S(1)}) custom-call(s32[1]{0:T(128)} %bitcast.me_ref.refs_0_, s32[3]{0:T(128)S(1)} %bitcast.14, s32[3]{0:T(128)S(1)} %bitcast.18, s32[1]{0:T(128)} %bitcast.8.refs_3_, ...), custom_call_target="tpu_custom_call" | custom-call | flops 10000000000 | bytes 1000000 | tf_op jit(solution)/shard_map/top/pallas_call | solution.py:351
  35.6 2.3 %back.1 = (f32[4,136,256]{2,1,0:T(8,128)}, f32[2,2,192,128]{3,2,1,0:T(8,128)S(1)}, f32[384,128]{1,0:T(8,128)S(1)}, f32[384,128]{1,0:T(8,128)S(1)}) custom-call(s32[1]{0:T(128)} %bitcast.me_ref.refs_0_, s32[3]{0:T(128)S(1)} %bitcast.15, s32[3]{0:T(128)S(1)} %bitcast.19, s32[1]{0:T(128)} %bitcast.9.refs_3_, ...), custom_call_target="tpu_custom_call" | custom-call | flops 6000000000 | bytes 1000000 | tf_op jit(solution)/shard_map/back/pallas_call | solution.py:351
  37.9 12.6 %all-to-all-start.1 = ((f32[4,136,256]{2,1,0:T(8,128)}), f32[4,136,256]{2,1,0:T(8,128)S(1)}, u32[]{:S(2)}, u32[]{:S(2)}) async-start(f32[4,136,256]{2,1,0:T(8,128)} %get-tuple-element.45), calls=%async_computation.1 | async-start | bytes 1114112 | tf_op jit(solution)/shard_map/all_to_all | solution.py:438
  50.6 0.7 collective-permute-start.5
  51.3 4.8 %collective-permute-start.4 = (f32[768,128]{1,0:T(8,128)S(1)}, f32[768,128]{1,0:T(8,128)S(1)}, u32[]{:S(2)}, u32[]{:S(2)}) collective-permute-start(f32[768,128]{1,0:T(8,128)S(1)} %pad_maximum_fusion), channel_id=1, source_target_pairs={{0,1},{2,3},{1,0},{3,2},{4,5},{6,7},{5,4},{7,6},{8,9},{10,11},{9,8... | collective-permute-start | bytes 1179656 | tf_op jit(solution)/shard_map/ppermute | solution.py:348
  56.1 8.2 %all-to-all-done.1.share_in = f32[4,136,256]{2,1,0:T(8,128)S(1)} async-done(((f32[4,136,256]{2,1,0:T(8,128)}), f32[4,136,256]{2,1,0:T(8,128)S(1)}, u32[]{:S(2)}, u32[]{:S(2)}) %all-to-all-start.1) | async-done | bytes 557088 | tf_op jit(solution)/shard_map/all_to_all | solution.py:438
  64.3 0.0 collective-permute-start.8
  64.3 1.5 %collective-permute-start.7 = (f32[8,128]{1,0:T(8,128)S(1)}, f32[8,128]{1,0:T(8,128)S(1)}, u32[]{:S(2)}, u32[]{:S(2)}) collective-permute-start(f32[8,128]{1,0:T(8,128)S(1)} %slice_reduce_fusion), channel_id=1, source_target_pairs={{0,8},{4,12},{8,0},{12,4},{16,24},{20,28},{24,16},{28,20},{1,9},{5... | collective-permute-start | bytes 12296 | tf_op jit(solution)/shard_map/ppermute | solution.py:328
  65.8 0.3 collective-permute-start.6
  66.1 1.2 %collective-permute-done.8 = f32[8,128]{1,0:T(8,128)S(1)} collective-permute-done((f32[8,128]{1,0:T(8,128)S(1)}, f32[8,128]{1,0:T(8,128)S(1)}, u32[]{:S(2)}, u32[]{:S(2)}) %collective-permute-start.8) | collective-permute-done | bytes 4128 | tf_op jit(solution)/shard_map/ppermute | solution.py:328
  67.3 0.6 collective-permute-done.7
  67.9 0.0 collective-permute-done.6
  67.9 4.3 %collective-permute-start.9 = (f32[8,128]{1,0:T(8,128)S(1)}, f32[8,128]{1,0:T(8,128)S(1)}, u32[]{:S(2)}, u32[]{:S(2)}) collective-permute-start(f32[8,128]{1,0:T(8,128)S(1)} %add_add_fusion), channel_id=1, source_target_pairs={{0,16},{4,20},{8,24},{12,28},{16,0},{20,4},{24,8},{28,12},{1,17},{... | collective-permute-start | bytes 12296 | tf_op jit(solution)/shard_map/ppermute | solution.py:328
  72.2 1.6 %collective-permute-done.9 = f32[8,128]{1,0:T(8,128)S(1)} collective-permute-done((f32[8,128]{1,0:T(8,128)S(1)}, f32[8,128]{1,0:T(8,128)S(1)}, u32[]{:S(2)}, u32[]{:S(2)}) %collective-permute-start.9) | collective-permute-done | bytes 4128 | tf_op jit(solution)/shard_map/ppermute | solution.py:328
  73.8 0.0 collective-permute-done.5.odd_in
  73.8 0.0 collective-permute-done.4.even_in
  73.8 1.2 %finish.1 = (f32[4,2,192,128]{3,2,1,0:T(8,128)}, f32[1,4,32,256]{3,2,1,0:T(8,128)}) custom-call(s32[1]{0:T(128)} %bitcast.me_ref.refs_0_, f32[2,2,192,128]{3,2,1,0:T(8,128)S(1)} %get-tuple-element.34.late_ref, f32[2,2,192,128]{3,2,1,0:T(8,128)S(1)} %get-tuple-element.40.early_ref, f32[768,128]{1,0:T(8,128)S(1)} %collective-permute-done.4.even_in, ...), custom_call_target="tpu_custom_call" | custom-call | bytes 1000000 | tf_op jit(solution)/shard_map/finish/pallas_call | solution.py:351
  (5 shorter events, 0.1 us)
Async XLA Ops:
  0.6 27.4 %copy-start.5 = (s32[1,1,3]{2,1,0:T(1,128)S(1)}, s32[1,1,3]{2,1,0:T(1,128)}, u32[]{:S(2)}) copy-start(s32[1,1,3]{2,1,0:T(1,128)} %param.10) | copy-start | bytes 40
  0.6 27.4 %copy-start.7 = (s32[1,1,3]{2,1,0:T(1,128)S(1)}, s32[1,1,3]{2,1,0:T(1,128)}, u32[]{:S(2)}) copy-start(s32[1,1,3]{2,1,0:T(1,128)} %param.11) | copy-start | bytes 40
  2.4 21.9 %all-to-all-start = ((f32[4,4,32,256]{3,2,1,0:T(8,128)}), f32[4,4,32,256]{3,2,1,0:T(8,128)S(1)}, u32[]{:S(2)}, u32[]{:S(2)}) async-start(f32[4,4,32,256]{3,2,1,0:T(8,128)} %broadcast_in_dim.8), calls=%async_computation | async-start | bytes 1048576 | tf_op jit(solution)/shard_map/all_to_all | solution.py:373
  9.4 1.1 %copy-start = (f32[4,2,192,128]{3,2,1,0:T(8,128)S(1)}, f32[4,2,192,128]{3,2,1,0:T(8,128)}, u32[]{:S(2)}) copy-start(f32[4,2,192,128]{3,2,1,0:T(8,128)} %potential_ref.3) | copy-start | bytes 2359300
  10.5 0.9 %copy-start.2 = (bf16[1,1,3,128,128]{4,3,2,1,0:T(8,128)(2,1)S(1)}, bf16[1,1,3,128,128]{4,3,2,1,0:T(8,128)(2,1)}, u32[]{:S(2)}) copy-start(bf16[1,1,3,128,128]{4,3,2,1,0:T(8,128)(2,1)} %param.9) | copy-start | bytes 294916
  11.4 0.7 copy-start.4
  12.1 0.7 copy-start.6
  13.6 14.5 %collective-permute-start.2 = (f32[392,128]{1,0:T(8,128)S(1)}, f32[392,128]{1,0:T(8,128)S(1)}, u32[]{:S(2)}, u32[]{:S(2)}) collective-permute-start(f32[392,128]{1,0:T(8,128)S(1)} %get-tuple-element.29), channel_id=1, source_target_pairs={{0,1},{2,3},{1,0},{3,2},{4,5},{6,7},{5,4},{7,6},{8,9},{10,11},{9,8... | collective-permute-start | bytes 602120 | tf_op jit(solution)/shard_map/ppermute | solution.py:348
  15.6 12.4 %collective-permute-start.3 = (f32[392,128]{1,0:T(8,128)S(1)}, f32[392,128]{1,0:T(8,128)S(1)}, u32[]{:S(2)}, u32[]{:S(2)}) collective-permute-start(f32[392,128]{1,0:T(8,128)S(1)} %get-tuple-element.30), channel_id=1, source_target_pairs={{1,2},{2,1},{5,6},{6,5},{9,10},{10,9},{13,14},{14,13},{17,18},{18,... | collective-permute-start | bytes 602120 | tf_op jit(solution)/shard_map/ppermute | solution.py:348
  16.3 15.9 %collective-permute-start = (f32[768,128]{1,0:T(8,128)S(1)}, f32[768,128]{1,0:T(8,128)S(1)}, u32[]{:S(2)}, u32[]{:S(2)}) collective-permute-start(f32[768,128]{1,0:T(8,128)S(1)} %get-tuple-element.26), channel_id=1, source_target_pairs={{0,1},{2,3},{1,0},{3,2},{4,5},{6,7},{5,4},{7,6},{8,9},{10,11},{9,8... | collective-permute-start | bytes 1179656 | tf_op jit(solution)/shard_map/ppermute | solution.py:348
  20.5 11.7 %collective-permute-start.1 = (f32[768,128]{1,0:T(8,128)S(1)}, f32[768,128]{1,0:T(8,128)S(1)}, u32[]{:S(2)}, u32[]{:S(2)}) collective-permute-start(f32[768,128]{1,0:T(8,128)S(1)} %get-tuple-element.27), channel_id=1, source_target_pairs={{1,2},{2,1},{5,6},{6,5},{9,10},{10,9},{13,14},{14,13},{17,18},{18,... | collective-permute-start | bytes 1179656 | tf_op jit(solution)/shard_map/ppermute | solution.py:348
  24.3 1.1 %copy-start.1 = (f32[4,2,192,128]{3,2,1,0:T(8,128)S(1)}, f32[4,2,192,128]{3,2,1,0:T(8,128)}, u32[]{:S(2)}) copy-start(f32[4,2,192,128]{3,2,1,0:T(8,128)} %potential_ref.3) | copy-start | bytes 2359300
  25.4 0.9 %copy-start.3 = (bf16[1,1,3,128,128]{4,3,2,1,0:T(8,128)(2,1)S(1)}, bf16[1,1,3,128,128]{4,3,2,1,0:T(8,128)(2,1)}, u32[]{:S(2)}) copy-start(bf16[1,1,3,128,128]{4,3,2,1,0:T(8,128)(2,1)} %param.9) | copy-start | bytes 294916
  26.3 1.2 %copy-start.8 = (bf16[8,256,256]{2,1,0:T(8,128)(2,1)S(1)}, bf16[8,256,256]{2,1,0:T(8,128)(2,1)}, u32[]{:S(2)}) copy-start(bf16[8,256,256]{2,1,0:T(8,128)(2,1)} %constant.8.clone.tables_ref) | copy-start | bytes 3145732
  37.9 26.3 %all-to-all-start.1 = ((f32[4,136,256]{2,1,0:T(8,128)}), f32[4,136,256]{2,1,0:T(8,128)S(1)}, u32[]{:S(2)}, u32[]{:S(2)}) async-start(f32[4,136,256]{2,1,0:T(8,128)} %get-tuple-element.45), calls=%async_computation.1 | async-start | bytes 1114112 | tf_op jit(solution)/shard_map/all_to_all | solution.py:438
  50.6 23.2 %collective-permute-start.5 = (f32[768,128]{1,0:T(8,128)S(1)}, f32[768,128]{1,0:T(8,128)S(1)}, u32[]{:S(2)}, u32[]{:S(2)}) collective-permute-start(f32[768,128]{1,0:T(8,128)S(1)} %pad_maximum_fusion.1), channel_id=1, source_target_pairs={{1,2},{2,1},{5,6},{6,5},{9,10},{10,9},{13,14},{14,13},{17,18},{18,... | collective-permute-start | bytes 1179656 | tf_op jit(solution)/shard_map/ppermute | solution.py:348
  51.3 22.4 %collective-permute-start.4 = (f32[768,128]{1,0:T(8,128)S(1)}, f32[768,128]{1,0:T(8,128)S(1)}, u32[]{:S(2)}, u32[]{:S(2)}) collective-permute-start(f32[768,128]{1,0:T(8,128)S(1)} %pad_maximum_fusion), channel_id=1, source_target_pairs={{0,1},{2,3},{1,0},{3,2},{4,5},{6,7},{5,4},{7,6},{8,9},{10,11},{9,8... | collective-permute-start | bytes 1179656 | tf_op jit(solution)/shard_map/ppermute | solution.py:348
  64.3 3.0 %collective-permute-start.8 = (f32[8,128]{1,0:T(8,128)S(1)}, f32[8,128]{1,0:T(8,128)S(1)}, u32[]{:S(2)}, u32[]{:S(2)}) collective-permute-start(f32[8,128]{1,0:T(8,128)S(1)} %slice_reduce_fusion), channel_id=1, source_target_pairs={{0,12},{4,8},{8,4},{12,0},{16,28},{20,24},{24,20},{28,16},{1,13},{... | collective-permute-start | bytes 12296 | tf_op jit(solution)/shard_map/ppermute | solution.py:328
  64.3 3.6 %collective-permute-start.7 = (f32[8,128]{1,0:T(8,128)S(1)}, f32[8,128]{1,0:T(8,128)S(1)}, u32[]{:S(2)}, u32[]{:S(2)}) collective-permute-start(f32[8,128]{1,0:T(8,128)S(1)} %slice_reduce_fusion), channel_id=1, source_target_pairs={{0,8},{4,12},{8,0},{12,4},{16,24},{20,28},{24,16},{28,20},{1,9},{5... | collective-permute-start | bytes 12296 | tf_op jit(solution)/shard_map/ppermute | solution.py:328
  65.8 2.1 %collective-permute-start.6 = (f32[8,128]{1,0:T(8,128)S(1)}, f32[8,128]{1,0:T(8,128)S(1)}, u32[]{:S(2)}, u32[]{:S(2)}) collective-permute-start(f32[8,128]{1,0:T(8,128)S(1)} %slice_reduce_fusion), channel_id=1, source_target_pairs={{0,4},{4,0},{8,12},{12,8},{16,20},{20,16},{24,28},{28,24},{1,5},{5... | collective-permute-start | bytes 12296 | tf_op jit(solution)/shard_map/ppermute | solution.py:328
  67.9 5.8 %collective-permute-start.9 = (f32[8,128]{1,0:T(8,128)S(1)}, f32[8,128]{1,0:T(8,128)S(1)}, u32[]{:S(2)}, u32[]{:S(2)}) collective-permute-start(f32[8,128]{1,0:T(8,128)S(1)} %add_add_fusion), channel_id=1, source_target_pairs={{0,16},{4,20},{8,24},{12,28},{16,0},{20,4},{24,8},{28,12},{1,17},{... | collective-permute-start | bytes 12296 | tf_op jit(solution)/shard_map/ppermute | solution.py:328
where the time goes:
time: 75.7 us; the launch traced here: 75 us
  starting transfers between devices  38.2 us (50%)
  waiting for transfers between devices  16.4 us (22%)
  Pallas kernels  10.6 us (14%)
  local copies, waits for them, and re-layouts  8.35 us (11%)
  between operations  1.42 us (2%)
    ppermute x6, starting transfers between devices, exchange(): return lax.ppermute(value, 'pos', edges + [(j, i) for i, j in edges])  13.1 us
    all_to_all x1, starting transfers between devices, body(): shares = lax.all_to_all(c['share'], 'pos', 0, 0)  12.6 us
    pallas_call x6, Pallas kernels, call(): pl.pallas_call(kernel, out_shape=[x[0] if isinstance(x, tuple) else x for...  10.6 us
    all_to_all x1, waiting for transfers between devices, body(): shares = lax.all_to_all(c['share'], 'pos', 0, 0)  8.15 us
    unnamed x18, local copies, waits for them, and re-layouts  6.59 us
    all_to_all x1, starting transfers between devices, body(): lax.all_to_all(jnp.broadcast_to(probe, (pieces,) + probe.shape[1:]), 'pos...  6.32 us
    ppermute x4, starting transfers between devices, total_over(): lax.ppermute(value, axis, [(i, i ^ step * k) for i in range(n)])  6.12 us
    ppermute x4, waiting for transfers between devices, total_over(): lax.ppermute(value, axis, [(i, i ^ step * k) for i in range(n)])  3.37 us
  transfers between devices with their start and end apart: 12, of which 6 were waited for; matrix products, arithmetic and copies ran while one was open for 0% of the time, Pallas kernels for 5%

commit v1 on v0

--- a/solution.py
+++ b/solution.py
@@ -124,6 +124,11 @@
     return magnitude * cosine(phase), magnitude * sine(phase)
 
 
+def spread_kernel(probe_ref, out_ref):
+    for k in range(out_ref.shape[0]):
+        out_ref[k] = probe_ref[0]
+
+
 def gate_kernel(*refs):
     pass
 
@@ -197,7 +202,7 @@
             r.amps_all[p] = r.amps[p].astype(jnp.float32)
             r.amps_all[slots + p] = halves(0, begin + p * size, size)[1]
     if back:
-        r.grads[...] = jnp.zeros_like(r.grads)
+        r.grads[:, 0:2] = jnp.zeros((len(back), 2) + r.grads.shape[2:], jnp.float32)
     if 0 in back:
         r.total[...] = jnp.zeros_like(r.total)
 
@@ -216,54 +221,69 @@
         ref = r.get("trans_%d" % s)
         return ref[at, 0], ref[at, 1]
 
-    def slot_step(at, misfit):
-        k = held[3 * at + 1]
-        row = held[3 * at + 2]
-        col = held[3 * at + 3]
-        own = k < slots
-        left = jnp.where(own, 0, 1)
-        right = jnp.where(own, jnp.where(last, 2, 1), 0)
-        turn = lax.rem(size - col, size)
-        inside = lanes >= col
+    def slot_step(ats, misfit):
+        about = [[held[3 * at + 1 + j] for j in range(3)] for at in ats]
+        rows_at = [pl.ds(row, size) for _, row, _ in about]
+        left = [jnp.where(k < slots, 0, 1) for k, _, _ in about]
+        right = [jnp.where(k < slots, jnp.where(last, 2, 1), 0) for k, _, _ in about]
+        inside = [lanes >= col for _, _, col in about]
+        every = range(len(ats))
+
+        def moved(waves, right_table, left_table):
+            flat = transform(sum(waves, []), right_table, left_table)
+            return [flat[j * modes : (j + 1) * modes] for j in every]
+
         for i, s in enumerate(ahead):
-            for c in range(2):
-                both = jnp.where(inside, r.tiles[i, left, c, pl.ds(row, size), :], r.tiles[i, right, c, pl.ds(row, size), :])
-                r.get("trans_%d" % s)[at, c] = pltpu.roll(both, turn, 1)
-            waves = [mul(trans(s, at), w) for w in psi(s, at)]
+            waves = []
+            for j in every:
+                turn = lax.rem(size - about[j][2], size)
+                for c in range(2):
+                    both = jnp.where(
+                        inside[j], r.tiles[i, left[j], c, rows_at[j], :], r.tiles[i, right[j], c, rows_at[j], :]
+                    )
+                    r.get("trans_%d" % s)[ats[j], c] = pltpu.roll(both, turn, 1)
+                waves.append([mul(trans(s, ats[j]), w) for w in psi(s, ats[j])])
             if top and s == ahead[-1]:
-                waves = transform(waves, r.tables[0], r.tables[4])
+                waves = moved(waves, r.tables[0], r.tables[4])
             else:
-                waves = transform(waves, r.tables[2], r.tables[6])
-                store(r.get("psi_%d" % (s + 1)), waves, at)
+                waves = moved(waves, r.tables[2], r.tables[6])
+                for j in every:
+                    store(r.get("psi_%d" % (s + 1)), waves[j], ats[j])
         if top:
-            inten = sum(re * re + im * im for re, im in waves)
-            model = jnp.sqrt(inten + REG)
-            observed = r.amps_all[k]
-            diff = model - observed
-            misfit = misfit + jnp.sum(diff * diff, axis=0, keepdims=True)
-            ratio = 1.0 - observed / model
-            waves = transform([(ratio * re, ratio * im) for re, im in waves], r.tables[1], r.tables[5])
+            for j in every:
+                inten = sum(re * re + im * im for re, im in waves[j])
+                model = jnp.sqrt(inten + REG)
+                observed = r.amps_all[about[j][0]]
+                diff = model - observed
+                misfit = misfit + jnp.sum(diff * diff, axis=0, keepdims=True)
+                ratio = 1.0 - observed / model
+                waves[j] = [(ratio * re, ratio * im) for re, im in waves[j]]
+            waves = moved(waves, r.tables[1], r.tables[5])
         elif back:
-            waves = load(r.wave_in, at)
+            waves = [load(r.wave_in, at) for at in ats]
         for i, s in enumerate(back):
-            waves = [mulc(trans(s, at), w) for w in waves]
-            quot = [mulc(a, w) for a, w in zip(psi(s, at), waves)]
-            values = sum(im for _, im in quot), -sum(re for re, _ in quot)
-            for c in range(2):
-                turned = pltpu.roll(values[c], col, 1)
-                r.grads[i, left, c, pl.ds(row, size), :] += jnp.where(inside, turned, 0.0)
-                r.grads[i, right, c, pl.ds(row, size), :] += jnp.where(inside, 0.0, turned)
+            for j in every:
+                waves[j] = [mulc(trans(s, ats[j]), w) for w in waves[j]]
+                quot = [mulc(a, w) for a, w in zip(psi(s, ats[j]), waves[j])]
+                values = sum(im for _, im in quot), -sum(re for re, _ in quot)
+                for c in range(2):
+                    turned = pltpu.roll(values[c], about[j][2], 1)
+                    r.grads[i, left[j], c, rows_at[j], :] += jnp.where(inside[j], turned, 0.0)
+                    r.grads[i, right[j], c, rows_at[j], :] += jnp.where(inside[j], 0.0, turned)
             if s > 0:
-                waves = transform(waves, r.tables[3], r.tables[7])
-        if 0 in back:
-            for m, (re, im) in enumerate(waves):
-                r.total[m, :, :size] += re
-                r.total[m, :, size:] += im
-        elif back or top:
-            store(r.wave_out, waves, at)
+                waves = moved(waves, r.tables[3], r.tables[7])
+        for j in every:
+            if 0 in back:
+                for m, (re, im) in enumerate(waves[j]):
+                    r.total[m, :, :size] += re
+                    r.total[m, :, size:] += im
+            elif back or top:
+                store(r.wave_out, waves[j], ats[j])
         return misfit
 
-    misfit = lax.fori_loop(0, number, slot_step, jnp.zeros((1, size), jnp.float32))
+    twos = number // 2
+    misfit = lax.fori_loop(0, twos, lambda i, m: slot_step([2 * i, 2 * i + 1], m), jnp.zeros((1, size), jnp.float32))
+    misfit = lax.fori_loop(2 * twos, number, lambda i, m: slot_step([i], m), misfit)
     if top:
         value = jnp.sum(misfit, axis=1, keepdims=True)
         lane = lax.broadcasted_iota(jnp.int32, (1, 1, size), 2)
@@ -370,7 +390,8 @@
         flops = (len(ahead) + len(back) + 1) * 2 * 10**9
         return dict(zip(made, call(kernel, list(given.values()), list(made.values()), name, scratch.values(), flops)))
 
-    gathered = lax.all_to_all(jnp.broadcast_to(probe, (pieces,) + probe.shape[1:]), "pos", 0, 0)
+    (spread,) = call(spread_kernel, [probe], [array((pieces,) + probe.shape[1:])], "spread")
+    gathered = lax.all_to_all(spread, "pos", 0, 0)
     heights = [len(groups[0]) * rows + 8, len(groups[1]) * rows + slots * size]
     packed = call(
         functools.partial(pack_kernel, groups),

time: 75.7 us -> 72.2 us (0.954)
  starting transfers between devices: 38.2 us -> 33.5 us
  Pallas kernels: 10.6 us -> 12.1 us
  local copies, waits for them, and re-layouts: 8.35 us -> 7.48 us
    all_to_all x1, starting transfers between devices: 12.6 us -> 9.16 us  [body(): shares = lax.all_to_all(c['share'], 'pos', 0, 0)]
    broadcast_in_dim x1 -> x0, local copies, waits for them, and re-layouts: 1.76 us -> none  [body(): jnp.broadcast_to(probe, (pieces,) + probe.shape[1:])]
    pallas_call x6 -> x7, Pallas kernels: 10.6 us -> 12.1 us  [call(): pl.pallas_call(kernel, out_shape=[x[0] if isinstance(x, tuple) else x for...]
    ppermute x4, starting transfers between devices: 6.12 us -> 4.95 us  [total_over(): lax.ppermute(value, axis, [(i, i ^ step * k) for i in range(n)])]
    unnamed x18 -> x20, local copies, waits for them, and re-layouts: 6.59 us -> 7.48 us
  transfers between devices with their start and end apart: 12 -> 12, of which waited for: 6 -> 5; matrix products, arithmetic and copies ran while one was open for 0% -> 0% of each run, Pallas kernels for 5% -> 5%
where the time goes in v1:
time: 72.2 us; the launch traced here: 71.6 us
  starting transfers between devices  33.5 us (46%)
  waiting for transfers between devices  17 us (24%)
  Pallas kernels  12.1 us (17%)
  local copies, waits for them, and re-layouts  7.48 us (10%)
  between operations  1.42 us (2%)
    ppermute x6, starting transfers between devices, exchange(): return lax.ppermute(value, 'pos', edges + [(j, i) for i, j in edges])  13.1 us
    pallas_call x7, Pallas kernels, call(): pl.pallas_call(kernel, out_shape=[x[0] if isinstance(x, tuple) else x for...  12.1 us
    all_to_all x1, starting transfers between devices, body(): shares = lax.all_to_all(c['share'], 'pos', 0, 0)  9.16 us
    all_to_all x1, waiting for transfers between devices, body(): shares = lax.all_to_all(c['share'], 'pos', 0, 0)  8.15 us
    unnamed x20, local copies, waits for them, and re-layouts  7.48 us
    all_to_all x1, starting transfers between devices, body(): gathered = lax.all_to_all(spread, 'pos', 0, 0)  6.32 us
    ppermute x4, starting transfers between devices, total_over(): lax.ppermute(value, axis, [(i, i ^ step * k) for i in range(n)])  4.95 us
    ppermute x4, waiting for transfers between devices, total_over(): lax.ppermute(value, axis, [(i, i ^ step * k) for i in range(n)])  4.04 us
  transfers between devices with their start and end apart: 12, of which 5 were waited for; matrix products, arithmetic and copies ran while one was open for 0% of the time, Pallas kernels for 5%

profile of v1, /device:TPU:0, one launch (start us, length us, event | category | flops | bytes accessed | tf_op | source)
XLA Modules:
  0.0 71.6 jit_solution(5593110952077593081)
XLA Ops:
  0.6 0.0 copy-start.2
  0.6 0.9 %copy-done.2 = f32[1,4,32,256]{3,2,1,0:T(8,128)S(1)} copy-done((f32[1,4,32,256]{3,2,1,0:T(8,128)S(1)}, f32[1,4,32,256]{3,2,1,0:T(8,128)}, u32[]{:S(2)}) %copy-start.2) | copy-done | bytes 131096
  1.5 0.0 copy-start.6
  1.5 0.0 copy-start.8
  1.5 0.8 %spread.1 = f32[4,4,32,256]{3,2,1,0:T(8,128)} custom-call(f32[1,4,32,256]{3,2,1,0:T(8,128)S(1)} %copy-done.2), custom_call_target="tpu_custom_call" | custom-call | bytes 1000000 | tf_op jit(solution)/shard_map/spread/pallas_call | solution.py:371
  2.4 6.3 %all-to-all-start = ((f32[4,4,32,256]{3,2,1,0:T(8,128)}), f32[4,4,32,256]{3,2,1,0:T(8,128)S(1)}, u32[]{:S(2)}, u32[]{:S(2)}) async-start(f32[4,4,32,256]{3,2,1,0:T(8,128)} %spread.1), calls=%async_computation | async-start | bytes 1048576 | tf_op jit(solution)/shard_map/all_to_all | solution.py:394
  9.3 0.0 copy-start
  9.3 1.1 %copy-done = f32[4,2,192,128]{3,2,1,0:T(8,128)S(1)} copy-done((f32[4,2,192,128]{3,2,1,0:T(8,128)S(1)}, f32[4,2,192,128]{3,2,1,0:T(8,128)}, u32[]{:S(2)}) %copy-start) | copy-done | bytes 786456
  10.5 0.0 copy-start.3
  10.5 0.9 %copy-done.3 = bf16[1,1,3,128,128]{4,3,2,1,0:T(8,128)(2,1)S(1)} copy-done((bf16[1,1,3,128,128]{4,3,2,1,0:T(8,128)(2,1)S(1)}, bf16[1,1,3,128,128]{4,3,2,1,0:T(8,128)(2,1)}, u32[]{:S(2)}) %copy-start.3) | copy-done | bytes 98328
  11.4 0.0 copy-start.5
  11.4 0.7 copy-done.5
  12.0 0.0 copy-start.7
  12.0 0.7 copy-done.7
  12.7 0.8 %pack.1 = (f32[392,128]{1,0:T(8,128)S(1)}, f32[392,128]{1,0:T(8,128)S(1)}, f32[768,128]{1,0:T(8,128)S(1)}, f32[768,128]{1,0:T(8,128)S(1)}) custom-call(s32[1]{0:T(128)} %bitcast.me_ref.refs_0_, s32[3]{0:T(128)S(1)} %bitcast.11, s32[3]{0:T(128)S(1)} %bitcast.15, s32[1]{0:T(128)} %bitcast.5.count_ref, f32[4,2,192,128]{3,2,1,0:T(8,128)S(1)} %copy-done, ...), custom_call_target="tpu_custom_call" | custom-call | bytes 1000000 | tf_op jit(solution)/shard_map/pack/pallas_call | solution.py:371
  13.5 2.1 %collective-permute-start.2 = (f32[392,128]{1,0:T(8,128)S(1)}, f32[392,128]{1,0:T(8,128)S(1)}, u32[]{:S(2)}, u32[]{:S(2)}) collective-permute-start(f32[392,128]{1,0:T(8,128)S(1)} %get-tuple-element.29), channel_id=1, source_target_pairs={{0,1},{2,3},{1,0},{3,2},{4,5},{6,7},{5,4},{7,6},{8,9},{10,11},{9,8... | collective-permute-start | bytes 602120 | tf_op jit(solution)/shard_map/ppermute | solution.py:368
  15.6 0.7 collective-permute-start.3
  16.3 4.2 %collective-permute-start = (f32[768,128]{1,0:T(8,128)S(1)}, f32[768,128]{1,0:T(8,128)S(1)}, u32[]{:S(2)}, u32[]{:S(2)}) collective-permute-start(f32[768,128]{1,0:T(8,128)S(1)} %get-tuple-element.26), channel_id=1, source_target_pairs={{0,1},{2,3},{1,0},{3,2},{4,5},{6,7},{5,4},{7,6},{8,9},{10,11},{9,8... | collective-permute-start | bytes 1179656 | tf_op jit(solution)/shard_map/ppermute | solution.py:368
  20.5 0.7 collective-permute-start.1
  21.2 3.0 %all-to-all-done.pieces_ref = f32[4,4,32,256]{3,2,1,0:T(8,128)S(1)} async-done(((f32[4,4,32,256]{3,2,1,0:T(8,128)}), f32[4,4,32,256]{3,2,1,0:T(8,128)S(1)}, u32[]{:S(2)}, u32[]{:S(2)}) %all-to-all-start) | async-done | bytes 524320 | tf_op jit(solution)/shard_map/all_to_all | solution.py:394
  24.2 0.0 copy-start.1
  24.2 1.1 %copy-done.1 = f32[4,2,192,128]{3,2,1,0:T(8,128)S(1)} copy-done((f32[4,2,192,128]{3,2,1,0:T(8,128)S(1)}, f32[4,2,192,128]{3,2,1,0:T(8,128)}, u32[]{:S(2)}) %copy-start.1) | copy-done | bytes 786456
  25.4 0.0 copy-start.4
  25.4 0.9 %copy-done.4 = bf16[1,1,3,128,128]{4,3,2,1,0:T(8,128)(2,1)S(1)} copy-done((bf16[1,1,3,128,128]{4,3,2,1,0:T(8,128)(2,1)S(1)}, bf16[1,1,3,128,128]{4,3,2,1,0:T(8,128)(2,1)}, u32[]{:S(2)}) %copy-start.4) | copy-done | bytes 98328
  26.3 0.0 copy-start.9
  26.3 1.2 %copy-done.9 = bf16[8,256,256]{2,1,0:T(8,128)(2,1)S(1)} copy-done((bf16[8,256,256]{2,1,0:T(8,128)(2,1)S(1)}, bf16[8,256,256]{2,1,0:T(8,128)(2,1)}, u32[]{:S(2)}) %copy-start.9) | copy-done | bytes 1048600
  27.5 0.5 prepare.1
  28.0 0.0 collective-permute-done.2.refs_6_
  28.0 0.0 collective-permute-done.3.refs_7_
  28.0 0.0 copy-done.6
  28.0 0.0 copy-done.8
  28.0 2.5 %ahead.1 = (s32[22]{0:T(128)S(1)}, f32[6,4,128,256]{3,2,1,0:T(8,128)S(1)}, f32[6,4,128,256]{3,2,1,0:T(8,128)S(1)}, f32[6,2,128,128]{3,2,1,0:T(8,128)S(1)}, f32[6,2,128,128]{3,2,1,0:T(8,128)S(1)}) custom-call(s32[1]{0:T(128)} %bitcast.me_ref.refs_0_, s32[3]{0:T(128)S(1)} %bitcast.12, s32[3]{0:T(128)S(1)} %bitcast.16, s32[1]{0:T(128)} %bitcast.6.refs_3_, ...), custom_call_target="tpu_custom_call" | custom-call | flops 6000000000 | bytes 1000000 | tf_op jit(solution)/shard_map/ahead/pallas_call | solution.py:371
  30.5 1.7 %collective-permute-done.refs_6_ = f32[768,128]{1,0:T(8,128)S(1)} collective-permute-done((f32[768,128]{1,0:T(8,128)S(1)}, f32[768,128]{1,0:T(8,128)S(1)}, u32[]{:S(2)}, u32[]{:S(2)}) %collective-permute-start) | collective-permute-done | bytes 393248 | tf_op jit(solution)/shard_map/ppermute | solution.py:368
  32.2 0.0 collective-permute-done.1.refs_7_
  32.2 3.7 %top.1 = (f32[8,128]{1,0:T(8,128)S(1)}, f32[6,4,128,256]{3,2,1,0:T(8,128)S(1)}, f32[2,2,192,128]{3,2,1,0:T(8,128)S(1)}, f32[384,128]{1,0:T(8,128)S(1)}, f32[384,128]{1,0:T(8,128)S(1)}) custom-call(s32[1]{0:T(128)} %bitcast.me_ref.refs_0_, s32[3]{0:T(128)S(1)} %bitcast.13, s32[3]{0:T(128)S(1)} %bitcast.17, s32[1]{0:T(128)} %bitcast.7.refs_3_, ...), custom_call_target="tpu_custom_call" | custom-call | flops 10000000000 | bytes 1000000 | tf_op jit(solution)/shard_map/top/pallas_call | solution.py:371
  35.9 2.6 %back.1 = (f32[4,136,256]{2,1,0:T(8,128)}, f32[2,2,192,128]{3,2,1,0:T(8,128)S(1)}, f32[384,128]{1,0:T(8,128)S(1)}, f32[384,128]{1,0:T(8,128)S(1)}) custom-call(s32[1]{0:T(128)} %bitcast.me_ref.refs_0_, s32[3]{0:T(128)S(1)} %bitcast.14, s32[3]{0:T(128)S(1)} %bitcast.18, s32[1]{0:T(128)} %bitcast.8.refs_3_, ...), custom_call_target="tpu_custom_call" | custom-call | flops 6000000000 | bytes 1000000 | tf_op jit(solution)/shard_map/back/pallas_call | solution.py:371
  38.6 9.2 %all-to-all-start.1 = ((f32[4,136,256]{2,1,0:T(8,128)}), f32[4,136,256]{2,1,0:T(8,128)S(1)}, u32[]{:S(2)}, u32[]{:S(2)}) async-start(f32[4,136,256]{2,1,0:T(8,128)} %get-tuple-element.45), calls=%async_computation.1 | async-start | bytes 1114112 | tf_op jit(solution)/shard_map/all_to_all | solution.py:459
  47.7 0.7 collective-permute-start.5
  48.5 4.8 %collective-permute-start.4 = (f32[768,128]{1,0:T(8,128)S(1)}, f32[768,128]{1,0:T(8,128)S(1)}, u32[]{:S(2)}, u32[]{:S(2)}) collective-permute-start(f32[768,128]{1,0:T(8,128)S(1)} %pad_maximum_fusion), channel_id=1, source_target_pairs={{0,1},{2,3},{1,0},{3,2},{4,5},{6,7},{5,4},{7,6},{8,9},{10,11},{9,8... | collective-permute-start | bytes 1179656 | tf_op jit(solution)/shard_map/ppermute | solution.py:368
  53.2 8.2 %all-to-all-done.1.share_in = f32[4,136,256]{2,1,0:T(8,128)S(1)} async-done(((f32[4,136,256]{2,1,0:T(8,128)}), f32[4,136,256]{2,1,0:T(8,128)S(1)}, u32[]{:S(2)}, u32[]{:S(2)}) %all-to-all-start.1) | async-done | bytes 557088 | tf_op jit(solution)/shard_map/all_to_all | solution.py:459
  61.4 0.0 collective-permute-start.8
  61.4 3.7 %collective-permute-start.7 = (f32[8,128]{1,0:T(8,128)S(1)}, f32[8,128]{1,0:T(8,128)S(1)}, u32[]{:S(2)}, u32[]{:S(2)}) collective-permute-start(f32[8,128]{1,0:T(8,128)S(1)} %slice_reduce_fusion), channel_id=1, source_target_pairs={{0,8},{4,12},{8,0},{12,4},{16,24},{20,28},{24,16},{28,20},{1,9},{5... | collective-permute-start | bytes 12296 | tf_op jit(solution)/shard_map/ppermute | solution.py:348
  65.1 0.1 collective-permute-start.6
  65.2 0.0 collective-permute-done.8
  65.2 1.5 %collective-permute-done.7 = f32[8,128]{1,0:T(8,128)S(1)} collective-permute-done((f32[8,128]{1,0:T(8,128)S(1)}, f32[8,128]{1,0:T(8,128)S(1)}, u32[]{:S(2)}, u32[]{:S(2)}) %collective-permute-start.7) | collective-permute-done | bytes 4128 | tf_op jit(solution)/shard_map/ppermute | solution.py:348
  66.7 0.0 collective-permute-done.6
  66.7 1.2 %collective-permute-start.9 = (f32[8,128]{1,0:T(8,128)S(1)}, f32[8,128]{1,0:T(8,128)S(1)}, u32[]{:S(2)}, u32[]{:S(2)}) collective-permute-start(f32[8,128]{1,0:T(8,128)S(1)} %add_add_fusion), channel_id=1, source_target_pairs={{0,16},{4,20},{8,24},{12,28},{16,0},{20,4},{24,8},{28,12},{1,17},{... | collective-permute-start | bytes 12296 | tf_op jit(solution)/shard_map/ppermute | solution.py:348
  67.9 2.5 %collective-permute-done.9 = f32[8,128]{1,0:T(8,128)S(1)} collective-permute-done((f32[8,128]{1,0:T(8,128)S(1)}, f32[8,128]{1,0:T(8,128)S(1)}, u32[]{:S(2)}, u32[]{:S(2)}) %collective-permute-start.9) | collective-permute-done | bytes 4128 | tf_op jit(solution)/shard_map/ppermute | solution.py:348
  70.4 0.0 collective-permute-done.5.odd_in
  70.4 0.0 collective-permute-done.4.even_in
  70.4 1.2 %finish.1 = (f32[4,2,192,128]{3,2,1,0:T(8,128)}, f32[1,4,32,256]{3,2,1,0:T(8,128)}) custom-call(s32[1]{0:T(128)} %bitcast.me_ref.refs_0_, f32[2,2,192,128]{3,2,1,0:T(8,128)S(1)} %get-tuple-element.34.late_ref, f32[2,2,192,128]{3,2,1,0:T(8,128)S(1)} %get-tuple-element.40.early_ref, f32[768,128]{1,0:T(8,128)S(1)} %collective-permute-done.4.even_in, ...), custom_call_target="tpu_custom_call" | custom-call | bytes 1000000 | tf_op jit(solution)/shard_map/finish/pallas_call | solution.py:371
  (5 shorter events, 0.1 us)
Async XLA Ops:
  0.6 0.9 %copy-start.2 = (f32[1,4,32,256]{3,2,1,0:T(8,128)S(1)}, f32[1,4,32,256]{3,2,1,0:T(8,128)}, u32[]{:S(2)}) copy-start(f32[1,4,32,256]{3,2,1,0:T(8,128)} %probe_ref.1) | copy-start | bytes 393220
  1.5 26.4 %copy-start.6 = (s32[1,1,3]{2,1,0:T(1,128)S(1)}, s32[1,1,3]{2,1,0:T(1,128)}, u32[]{:S(2)}) copy-start(s32[1,1,3]{2,1,0:T(1,128)} %param.10) | copy-start | bytes 40
  1.5 26.5 %copy-start.8 = (s32[1,1,3]{2,1,0:T(1,128)S(1)}, s32[1,1,3]{2,1,0:T(1,128)}, u32[]{:S(2)}) copy-start(s32[1,1,3]{2,1,0:T(1,128)} %param.11) | copy-start | bytes 40
  2.4 21.9 %all-to-all-start = ((f32[4,4,32,256]{3,2,1,0:T(8,128)}), f32[4,4,32,256]{3,2,1,0:T(8,128)S(1)}, u32[]{:S(2)}, u32[]{:S(2)}) async-start(f32[4,4,32,256]{3,2,1,0:T(8,128)} %spread.1), calls=%async_computation | async-start | bytes 1048576 | tf_op jit(solution)/shard_map/all_to_all | solution.py:394
  9.3 1.1 %copy-start = (f32[4,2,192,128]{3,2,1,0:T(8,128)S(1)}, f32[4,2,192,128]{3,2,1,0:T(8,128)}, u32[]{:S(2)}) copy-start(f32[4,2,192,128]{3,2,1,0:T(8,128)} %potential_ref.3) | copy-start | bytes 2359300
  10.5 0.9 %copy-start.3 = (bf16[1,1,3,128,128]{4,3,2,1,0:T(8,128)(2,1)S(1)}, bf16[1,1,3,128,128]{4,3,2,1,0:T(8,128)(2,1)}, u32[]{:S(2)}) copy-start(bf16[1,1,3,128,128]{4,3,2,1,0:T(8,128)(2,1)} %param.9) | copy-start | bytes 294916
  11.4 0.7 copy-start.5
  12.0 0.7 copy-start.7
  13.5 14.5 %collective-permute-start.2 = (f32[392,128]{1,0:T(8,128)S(1)}, f32[392,128]{1,0:T(8,128)S(1)}, u32[]{:S(2)}, u32[]{:S(2)}) collective-permute-start(f32[392,128]{1,0:T(8,128)S(1)} %get-tuple-element.29), channel_id=1, source_target_pairs={{0,1},{2,3},{1,0},{3,2},{4,5},{6,7},{5,4},{7,6},{8,9},{10,11},{9,8... | collective-permute-start | bytes 602120 | tf_op jit(solution)/shard_map/ppermute | solution.py:368
  15.6 12.4 %collective-permute-start.3 = (f32[392,128]{1,0:T(8,128)S(1)}, f32[392,128]{1,0:T(8,128)S(1)}, u32[]{:S(2)}, u32[]{:S(2)}) collective-permute-start(f32[392,128]{1,0:T(8,128)S(1)} %get-tuple-element.30), channel_id=1, source_target_pairs={{1,2},{2,1},{5,6},{6,5},{9,10},{10,9},{13,14},{14,13},{17,18},{18,... | collective-permute-start | bytes 602120 | tf_op jit(solution)/shard_map/ppermute | solution.py:368
  16.3 15.9 %collective-permute-start = (f32[768,128]{1,0:T(8,128)S(1)}, f32[768,128]{1,0:T(8,128)S(1)}, u32[]{:S(2)}, u32[]{:S(2)}) collective-permute-start(f32[768,128]{1,0:T(8,128)S(1)} %get-tuple-element.26), channel_id=1, source_target_pairs={{0,1},{2,3},{1,0},{3,2},{4,5},{6,7},{5,4},{7,6},{8,9},{10,11},{9,8... | collective-permute-start | bytes 1179656 | tf_op jit(solution)/shard_map/ppermute | solution.py:368
  20.5 11.7 %collective-permute-start.1 = (f32[768,128]{1,0:T(8,128)S(1)}, f32[768,128]{1,0:T(8,128)S(1)}, u32[]{:S(2)}, u32[]{:S(2)}) collective-permute-start(f32[768,128]{1,0:T(8,128)S(1)} %get-tuple-element.27), channel_id=1, source_target_pairs={{1,2},{2,1},{5,6},{6,5},{9,10},{10,9},{13,14},{14,13},{17,18},{18,... | collective-permute-start | bytes 1179656 | tf_op jit(solution)/shard_map/ppermute | solution.py:368
  24.2 1.1 %copy-start.1 = (f32[4,2,192,128]{3,2,1,0:T(8,128)S(1)}, f32[4,2,192,128]{3,2,1,0:T(8,128)}, u32[]{:S(2)}) copy-start(f32[4,2,192,128]{3,2,1,0:T(8,128)} %potential_ref.3) | copy-start | bytes 2359300
  25.4 0.9 %copy-start.4 = (bf16[1,1,3,128,128]{4,3,2,1,0:T(8,128)(2,1)S(1)}, bf16[1,1,3,128,128]{4,3,2,1,0:T(8,128)(2,1)}, u32[]{:S(2)}) copy-start(bf16[1,1,3,128,128]{4,3,2,1,0:T(8,128)(2,1)} %param.9) | copy-start | bytes 294916
  26.3 1.2 %copy-start.9 = (bf16[8,256,256]{2,1,0:T(8,128)(2,1)S(1)}, bf16[8,256,256]{2,1,0:T(8,128)(2,1)}, u32[]{:S(2)}) copy-start(bf16[8,256,256]{2,1,0:T(8,128)(2,1)} %constant.8.clone.tables_ref) | copy-start | bytes 3145732
  38.6 22.8 %all-to-all-start.1 = ((f32[4,136,256]{2,1,0:T(8,128)}), f32[4,136,256]{2,1,0:T(8,128)S(1)}, u32[]{:S(2)}, u32[]{:S(2)}) async-start(f32[4,136,256]{2,1,0:T(8,128)} %get-tuple-element.45), calls=%async_computation.1 | async-start | bytes 1114112 | tf_op jit(solution)/shard_map/all_to_all | solution.py:459
  47.7 22.7 %collective-permute-start.5 = (f32[768,128]{1,0:T(8,128)S(1)}, f32[768,128]{1,0:T(8,128)S(1)}, u32[]{:S(2)}, u32[]{:S(2)}) collective-permute-start(f32[768,128]{1,0:T(8,128)S(1)} %pad_maximum_fusion.1), channel_id=1, source_target_pairs={{1,2},{2,1},{5,6},{6,5},{9,10},{10,9},{13,14},{14,13},{17,18},{18,... | collective-permute-start | bytes 1179656 | tf_op jit(solution)/shard_map/ppermute | solution.py:368
  48.5 21.9 %collective-permute-start.4 = (f32[768,128]{1,0:T(8,128)S(1)}, f32[768,128]{1,0:T(8,128)S(1)}, u32[]{:S(2)}, u32[]{:S(2)}) collective-permute-start(f32[768,128]{1,0:T(8,128)S(1)} %pad_maximum_fusion), channel_id=1, source_target_pairs={{0,1},{2,3},{1,0},{3,2},{4,5},{6,7},{5,4},{7,6},{8,9},{10,11},{9,8... | collective-permute-start | bytes 1179656 | tf_op jit(solution)/shard_map/ppermute | solution.py:368
  61.4 3.8 %collective-permute-start.8 = (f32[8,128]{1,0:T(8,128)S(1)}, f32[8,128]{1,0:T(8,128)S(1)}, u32[]{:S(2)}, u32[]{:S(2)}) collective-permute-start(f32[8,128]{1,0:T(8,128)S(1)} %slice_reduce_fusion), channel_id=1, source_target_pairs={{0,12},{4,8},{8,4},{12,0},{16,28},{20,24},{24,20},{28,16},{1,13},{... | collective-permute-start | bytes 12296 | tf_op jit(solution)/shard_map/ppermute | solution.py:348
  61.4 5.3 %collective-permute-start.7 = (f32[8,128]{1,0:T(8,128)S(1)}, f32[8,128]{1,0:T(8,128)S(1)}, u32[]{:S(2)}, u32[]{:S(2)}) collective-permute-start(f32[8,128]{1,0:T(8,128)S(1)} %slice_reduce_fusion), channel_id=1, source_target_pairs={{0,8},{4,12},{8,0},{12,4},{16,24},{20,28},{24,16},{28,20},{1,9},{5... | collective-permute-start | bytes 12296 | tf_op jit(solution)/shard_map/ppermute | solution.py:348
  65.1 1.6 %collective-permute-start.6 = (f32[8,128]{1,0:T(8,128)S(1)}, f32[8,128]{1,0:T(8,128)S(1)}, u32[]{:S(2)}, u32[]{:S(2)}) collective-permute-start(f32[8,128]{1,0:T(8,128)S(1)} %slice_reduce_fusion), channel_id=1, source_target_pairs={{0,4},{4,0},{8,12},{12,8},{16,20},{20,16},{24,28},{28,24},{1,5},{5... | collective-permute-start | bytes 12296 | tf_op jit(solution)/shard_map/ppermute | solution.py:348
  66.7 3.7 %collective-permute-start.9 = (f32[8,128]{1,0:T(8,128)S(1)}, f32[8,128]{1,0:T(8,128)S(1)}, u32[]{:S(2)}, u32[]{:S(2)}) collective-permute-start(f32[8,128]{1,0:T(8,128)S(1)} %add_add_fusion), channel_id=1, source_target_pairs={{0,16},{4,20},{8,24},{12,28},{16,0},{20,4},{24,8},{28,12},{1,17},{... | collective-permute-start | bytes 12296 | tf_op jit(solution)/shard_map/ppermute | solution.py:348

commit v2 on v1

--- a/solution.py
+++ b/solution.py
@@ -281,9 +281,19 @@
                 store(r.wave_out, waves[j], ats[j])
         return misfit
 
-    twos = number // 2
-    misfit = lax.fori_loop(0, twos, lambda i, m: slot_step([2 * i, 2 * i + 1], m), jnp.zeros((1, size), jnp.float32))
-    misfit = lax.fori_loop(2 * twos, number, lambda i, m: slot_step([i], m), misfit)
+    misfit = jnp.zeros((1, size), jnp.float32)
+    fives = jnp.where(number > 6, number // 5, (number == 5).astype(jnp.int32))
+    begin = 5 * fives
+    rest = number - begin
+    steps = [(rest == width).astype(jnp.int32) for width in range(1, 5)] + [fives]
+    steps[2] += 2 * (rest == 6).astype(jnp.int32)
+    for width, count in zip(range(1, 6), steps):
+        first = 0 if width == 5 else begin
+
+        def step(i, total, width=width, first=first):
+            return slot_step([first + width * i + j for j in range(width)], total)
+
+        misfit = lax.fori_loop(0, count, step, misfit)
     if top:
         value = jnp.sum(misfit, axis=1, keepdims=True)
         lane = lax.broadcasted_iota(jnp.int32, (1, 1, size), 2)

time: 72.2 us -> 70.6 us (0.978)
  starting transfers between devices: 33.5 us -> 31.5 us
  waiting for transfers between devices: 17 us -> 18.1 us
    all_to_all x1, starting transfers between devices: 9.16 us -> 6.25 us  [body(): shares = lax.all_to_all(c['share'], 'pos', 0, 0)]
    all_to_all x1, waiting for transfers between devices: 8.15 us -> 9.95 us  [body(): shares = lax.all_to_all(c['share'], 'pos', 0, 0)]
    ppermute x4, starting transfers between devices: 4.95 us -> 5.81 us  [total_over(): lax.ppermute(value, axis, [(i, i ^ step * k) for i in range(n)])]
where the time goes in v2:
time: 70.6 us; the launch traced here: 70.4 us
  starting transfers between devices  31.5 us (45%)
  waiting for transfers between devices  18.1 us (26%)
  Pallas kernels  11.8 us (17%)
  local copies, waits for them, and re-layouts  7.48 us (11%)
  between operations  1.42 us (2%)
    ppermute x6, starting transfers between devices, exchange(): return lax.ppermute(value, 'pos', edges + [(j, i) for i, j in edges])  13.1 us
    pallas_call x7, Pallas kernels, call(): pl.pallas_call(kernel, out_shape=[x[0] if isinstance(x, tuple) else x for...  11.8 us
    all_to_all x1, waiting for transfers between devices, body(): shares = lax.all_to_all(c['share'], 'pos', 0, 0)  9.95 us
    unnamed x20, local copies, waits for them, and re-layouts  7.48 us
    all_to_all x1, starting transfers between devices, body(): gathered = lax.all_to_all(spread, 'pos', 0, 0)  6.32 us
    all_to_all x1, starting transfers between devices, body(): shares = lax.all_to_all(c['share'], 'pos', 0, 0)  6.25 us
    ppermute x4, starting transfers between devices, total_over(): lax.ppermute(value, axis, [(i, i ^ step * k) for i in range(n)])  5.81 us
    ppermute x4, waiting for transfers between devices, total_over(): lax.ppermute(value, axis, [(i, i ^ step * k) for i in range(n)])  3.33 us
  transfers between devices with their start and end apart: 12, of which 5 were waited for; matrix products, arithmetic and copies ran while one was open for 0% of the time, Pallas kernels for 5%

profile of v2, /device:TPU:0, one launch (start us, length us, event | category | flops | bytes accessed | tf_op | source)
XLA Modules:
  0.0 70.4 jit_solution(5281076810039924948)
XLA Ops:
  0.6 0.0 copy-start.2
  0.6 0.9 %copy-done.2 = f32[1,4,32,256]{3,2,1,0:T(8,128)S(1)} copy-done((f32[1,4,32,256]{3,2,1,0:T(8,128)S(1)}, f32[1,4,32,256]{3,2,1,0:T(8,128)}, u32[]{:S(2)}) %copy-start.2) | copy-done | bytes 131096
  1.5 0.0 copy-start.6
  1.5 0.0 copy-start.8
  1.5 0.8 %spread.1 = f32[4,4,32,256]{3,2,1,0:T(8,128)} custom-call(f32[1,4,32,256]{3,2,1,0:T(8,128)S(1)} %copy-done.2), custom_call_target="tpu_custom_call" | custom-call | bytes 1000000 | tf_op jit(solution)/shard_map/spread/pallas_call | solution.py:381
  2.4 6.3 %all-to-all-start = ((f32[4,4,32,256]{3,2,1,0:T(8,128)}), f32[4,4,32,256]{3,2,1,0:T(8,128)S(1)}, u32[]{:S(2)}, u32[]{:S(2)}) async-start(f32[4,4,32,256]{3,2,1,0:T(8,128)} %spread.1), calls=%async_computation | async-start | bytes 1048576 | tf_op jit(solution)/shard_map/all_to_all | solution.py:404
  9.3 0.0 copy-start
  9.3 1.1 %copy-done = f32[4,2,192,128]{3,2,1,0:T(8,128)S(1)} copy-done((f32[4,2,192,128]{3,2,1,0:T(8,128)S(1)}, f32[4,2,192,128]{3,2,1,0:T(8,128)}, u32[]{:S(2)}) %copy-start) | copy-done | bytes 786456
  10.5 0.0 copy-start.3
  10.5 0.9 %copy-done.3 = bf16[1,1,3,128,128]{4,3,2,1,0:T(8,128)(2,1)S(1)} copy-done((bf16[1,1,3,128,128]{4,3,2,1,0:T(8,128)(2,1)S(1)}, bf16[1,1,3,128,128]{4,3,2,1,0:T(8,128)(2,1)}, u32[]{:S(2)}) %copy-start.3) | copy-done | bytes 98328
  11.4 0.0 copy-start.5
  11.4 0.7 copy-done.5
  12.0 0.0 copy-start.7
  12.0 0.7 copy-done.7
  12.7 0.8 %pack.1 = (f32[392,128]{1,0:T(8,128)S(1)}, f32[392,128]{1,0:T(8,128)S(1)}, f32[768,128]{1,0:T(8,128)S(1)}, f32[768,128]{1,0:T(8,128)S(1)}) custom-call(s32[1]{0:T(128)} %bitcast.me_ref.refs_0_, s32[3]{0:T(128)S(1)} %bitcast.11, s32[3]{0:T(128)S(1)} %bitcast.15, s32[1]{0:T(128)} %bitcast.5.count_ref, f32[4,2,192,128]{3,2,1,0:T(8,128)S(1)} %copy-done, ...), custom_call_target="tpu_custom_call" | custom-call | bytes 1000000 | tf_op jit(solution)/shard_map/pack/pallas_call | solution.py:381
  13.5 2.1 %collective-permute-start.2 = (f32[392,128]{1,0:T(8,128)S(1)}, f32[392,128]{1,0:T(8,128)S(1)}, u32[]{:S(2)}, u32[]{:S(2)}) collective-permute-start(f32[392,128]{1,0:T(8,128)S(1)} %get-tuple-element.29), channel_id=1, source_target_pairs={{0,1},{2,3},{1,0},{3,2},{4,5},{6,7},{5,4},{7,6},{8,9},{10,11},{9,8... | collective-permute-start | bytes 602120 | tf_op jit(solution)/shard_map/ppermute | solution.py:378
  15.6 0.7 collective-permute-start.3
  16.3 4.2 %collective-permute-start = (f32[768,128]{1,0:T(8,128)S(1)}, f32[768,128]{1,0:T(8,128)S(1)}, u32[]{:S(2)}, u32[]{:S(2)}) collective-permute-start(f32[768,128]{1,0:T(8,128)S(1)} %get-tuple-element.26), channel_id=1, source_target_pairs={{0,1},{2,3},{1,0},{3,2},{4,5},{6,7},{5,4},{7,6},{8,9},{10,11},{9,8... | collective-permute-start | bytes 1179656 | tf_op jit(solution)/shard_map/ppermute | solution.py:378
  20.5 0.7 collective-permute-start.1
  21.2 3.0 %all-to-all-done.pieces_ref = f32[4,4,32,256]{3,2,1,0:T(8,128)S(1)} async-done(((f32[4,4,32,256]{3,2,1,0:T(8,128)}), f32[4,4,32,256]{3,2,1,0:T(8,128)S(1)}, u32[]{:S(2)}, u32[]{:S(2)}) %all-to-all-start) | async-done | bytes 524320 | tf_op jit(solution)/shard_map/all_to_all | solution.py:404
  24.2 0.0 copy-start.1
  24.2 1.1 %copy-done.1 = f32[4,2,192,128]{3,2,1,0:T(8,128)S(1)} copy-done((f32[4,2,192,128]{3,2,1,0:T(8,128)S(1)}, f32[4,2,192,128]{3,2,1,0:T(8,128)}, u32[]{:S(2)}) %copy-start.1) | copy-done | bytes 786456
  25.4 0.0 copy-start.4
  25.4 0.9 %copy-done.4 = bf16[1,1,3,128,128]{4,3,2,1,0:T(8,128)(2,1)S(1)} copy-done((bf16[1,1,3,128,128]{4,3,2,1,0:T(8,128)(2,1)S(1)}, bf16[1,1,3,128,128]{4,3,2,1,0:T(8,128)(2,1)}, u32[]{:S(2)}) %copy-start.4) | copy-done | bytes 98328
  26.3 0.0 copy-start.9
  26.3 1.2 %copy-done.9 = bf16[8,256,256]{2,1,0:T(8,128)(2,1)S(1)} copy-done((bf16[8,256,256]{2,1,0:T(8,128)(2,1)S(1)}, bf16[8,256,256]{2,1,0:T(8,128)(2,1)}, u32[]{:S(2)}) %copy-start.9) | copy-done | bytes 1048600
  27.5 0.5 prepare.1
  28.0 0.0 collective-permute-done.2.refs_6_
  28.0 0.0 collective-permute-done.3.refs_7_
  28.0 0.0 copy-done.6
  28.0 0.0 copy-done.8
  28.0 2.4 %ahead.1 = (s32[22]{0:T(128)S(1)}, f32[6,4,128,256]{3,2,1,0:T(8,128)S(1)}, f32[6,4,128,256]{3,2,1,0:T(8,128)S(1)}, f32[6,2,128,128]{3,2,1,0:T(8,128)S(1)}, f32[6,2,128,128]{3,2,1,0:T(8,128)S(1)}) custom-call(s32[1]{0:T(128)} %bitcast.me_ref.refs_0_, s32[3]{0:T(128)S(1)} %bitcast.12, s32[3]{0:T(128)S(1)} %bitcast.16, s32[1]{0:T(128)} %bitcast.6.refs_3_, ...), custom_call_target="tpu_custom_call" | custom-call | flops 6000000000 | bytes 1000000 | tf_op jit(solution)/shard_map/ahead/pallas_call | solution.py:381
  30.4 1.8 %collective-permute-done.refs_6_ = f32[768,128]{1,0:T(8,128)S(1)} collective-permute-done((f32[768,128]{1,0:T(8,128)S(1)}, f32[768,128]{1,0:T(8,128)S(1)}, u32[]{:S(2)}, u32[]{:S(2)}) %collective-permute-start) | collective-permute-done | bytes 393248 | tf_op jit(solution)/shard_map/ppermute | solution.py:378
  32.2 0.0 collective-permute-done.1.refs_7_
  32.2 3.5 %top.1 = (f32[8,128]{1,0:T(8,128)S(1)}, f32[6,4,128,256]{3,2,1,0:T(8,128)S(1)}, f32[2,2,192,128]{3,2,1,0:T(8,128)S(1)}, f32[384,128]{1,0:T(8,128)S(1)}, f32[384,128]{1,0:T(8,128)S(1)}) custom-call(s32[1]{0:T(128)} %bitcast.me_ref.refs_0_, s32[3]{0:T(128)S(1)} %bitcast.13, s32[3]{0:T(128)S(1)} %bitcast.17, s32[1]{0:T(128)} %bitcast.7.refs_3_, ...), custom_call_target="tpu_custom_call" | custom-call | flops 10000000000 | bytes 1000000 | tf_op jit(solution)/shard_map/top/pallas_call | solution.py:381
  35.7 2.5 %back.1 = (f32[4,136,256]{2,1,0:T(8,128)}, f32[2,2,192,128]{3,2,1,0:T(8,128)S(1)}, f32[384,128]{1,0:T(8,128)S(1)}, f32[384,128]{1,0:T(8,128)S(1)}) custom-call(s32[1]{0:T(128)} %bitcast.me_ref.refs_0_, s32[3]{0:T(128)S(1)} %bitcast.14, s32[3]{0:T(128)S(1)} %bitcast.18, s32[1]{0:T(128)} %bitcast.8.refs_3_, ...), custom_call_target="tpu_custom_call" | custom-call | flops 6000000000 | bytes 1000000 | tf_op jit(solution)/shard_map/back/pallas_call | solution.py:381
  38.3 6.2 %all-to-all-start.1 = ((f32[4,136,256]{2,1,0:T(8,128)}), f32[4,136,256]{2,1,0:T(8,128)S(1)}, u32[]{:S(2)}, u32[]{:S(2)}) async-start(f32[4,136,256]{2,1,0:T(8,128)} %get-tuple-element.45), calls=%async_computation.1 | async-start | bytes 1114112 | tf_op jit(solution)/shard_map/all_to_all | solution.py:469
  44.6 0.7 collective-permute-start.5
  45.3 4.8 %collective-permute-start.4 = (f32[768,128]{1,0:T(8,128)S(1)}, f32[768,128]{1,0:T(8,128)S(1)}, u32[]{:S(2)}, u32[]{:S(2)}) collective-permute-start(f32[768,128]{1,0:T(8,128)S(1)} %pad_maximum_fusion), channel_id=1, source_target_pairs={{0,1},{2,3},{1,0},{3,2},{4,5},{6,7},{5,4},{7,6},{8,9},{10,11},{9,8... | collective-permute-start | bytes 1179656 | tf_op jit(solution)/shard_map/ppermute | solution.py:378
  50.1 9.9 %all-to-all-done.1.share_in = f32[4,136,256]{2,1,0:T(8,128)S(1)} async-done(((f32[4,136,256]{2,1,0:T(8,128)}), f32[4,136,256]{2,1,0:T(8,128)S(1)}, u32[]{:S(2)}, u32[]{:S(2)}) %all-to-all-start.1) | async-done | bytes 557088 | tf_op jit(solution)/shard_map/all_to_all | solution.py:469
  60.0 0.0 collective-permute-start.8
  60.0 3.9 %collective-permute-start.7 = (f32[8,128]{1,0:T(8,128)S(1)}, f32[8,128]{1,0:T(8,128)S(1)}, u32[]{:S(2)}, u32[]{:S(2)}) collective-permute-start(f32[8,128]{1,0:T(8,128)S(1)} %slice_reduce_fusion), channel_id=1, source_target_pairs={{0,8},{4,12},{8,0},{12,4},{16,24},{20,28},{24,16},{28,20},{1,9},{5... | collective-permute-start | bytes 12296 | tf_op jit(solution)/shard_map/ppermute | solution.py:358
  63.9 0.1 collective-permute-start.6
  64.0 0.0 collective-permute-done.8
  64.0 1.5 %collective-permute-done.7 = f32[8,128]{1,0:T(8,128)S(1)} collective-permute-done((f32[8,128]{1,0:T(8,128)S(1)}, f32[8,128]{1,0:T(8,128)S(1)}, u32[]{:S(2)}, u32[]{:S(2)}) %collective-permute-start.7) | collective-permute-done | bytes 4128 | tf_op jit(solution)/shard_map/ppermute | solution.py:358
  65.5 0.0 collective-permute-done.6
  65.5 1.9 %collective-permute-start.9 = (f32[8,128]{1,0:T(8,128)S(1)}, f32[8,128]{1,0:T(8,128)S(1)}, u32[]{:S(2)}, u32[]{:S(2)}) collective-permute-start(f32[8,128]{1,0:T(8,128)S(1)} %add_add_fusion), channel_id=1, source_target_pairs={{0,16},{4,20},{8,24},{12,28},{16,0},{20,4},{24,8},{28,12},{1,17},{... | collective-permute-start | bytes 12296 | tf_op jit(solution)/shard_map/ppermute | solution.py:358
  67.4 1.8 %collective-permute-done.9 = f32[8,128]{1,0:T(8,128)S(1)} collective-permute-done((f32[8,128]{1,0:T(8,128)S(1)}, f32[8,128]{1,0:T(8,128)S(1)}, u32[]{:S(2)}, u32[]{:S(2)}) %collective-permute-start.9) | collective-permute-done | bytes 4128 | tf_op jit(solution)/shard_map/ppermute | solution.py:358
  69.2 0.0 collective-permute-done.5.odd_in
  69.2 0.0 collective-permute-done.4.even_in
  69.2 1.2 %finish.1 = (f32[4,2,192,128]{3,2,1,0:T(8,128)}, f32[1,4,32,256]{3,2,1,0:T(8,128)}) custom-call(s32[1]{0:T(128)} %bitcast.me_ref.refs_0_, f32[2,2,192,128]{3,2,1,0:T(8,128)S(1)} %get-tuple-element.34.late_ref, f32[2,2,192,128]{3,2,1,0:T(8,128)S(1)} %get-tuple-element.40.early_ref, f32[768,128]{1,0:T(8,128)S(1)} %collective-permute-done.4.even_in, ...), custom_call_target="tpu_custom_call" | custom-call | bytes 1000000 | tf_op jit(solution)/shard_map/finish/pallas_call | solution.py:381
  (5 shorter events, 0.1 us)
Async XLA Ops:
  0.6 0.9 %copy-start.2 = (f32[1,4,32,256]{3,2,1,0:T(8,128)S(1)}, f32[1,4,32,256]{3,2,1,0:T(8,128)}, u32[]{:S(2)}) copy-start(f32[1,4,32,256]{3,2,1,0:T(8,128)} %probe_ref.1) | copy-start | bytes 393220
  1.5 26.4 %copy-start.6 = (s32[1,1,3]{2,1,0:T(1,128)S(1)}, s32[1,1,3]{2,1,0:T(1,128)}, u32[]{:S(2)}) copy-start(s32[1,1,3]{2,1,0:T(1,128)} %param.10) | copy-start | bytes 40
  1.5 26.5 %copy-start.8 = (s32[1,1,3]{2,1,0:T(1,128)S(1)}, s32[1,1,3]{2,1,0:T(1,128)}, u32[]{:S(2)}) copy-start(s32[1,1,3]{2,1,0:T(1,128)} %param.11) | copy-start | bytes 40
  2.4 21.9 %all-to-all-start = ((f32[4,4,32,256]{3,2,1,0:T(8,128)}), f32[4,4,32,256]{3,2,1,0:T(8,128)S(1)}, u32[]{:S(2)}, u32[]{:S(2)}) async-start(f32[4,4,32,256]{3,2,1,0:T(8,128)} %spread.1), calls=%async_computation | async-start | bytes 1048576 | tf_op jit(solution)/shard_map/all_to_all | solution.py:404
  9.3 1.1 %copy-start = (f32[4,2,192,128]{3,2,1,0:T(8,128)S(1)}, f32[4,2,192,128]{3,2,1,0:T(8,128)}, u32[]{:S(2)}) copy-start(f32[4,2,192,128]{3,2,1,0:T(8,128)} %potential_ref.3) | copy-start | bytes 2359300
  10.5 0.9 %copy-start.3 = (bf16[1,1,3,128,128]{4,3,2,1,0:T(8,128)(2,1)S(1)}, bf16[1,1,3,128,128]{4,3,2,1,0:T(8,128)(2,1)}, u32[]{:S(2)}) copy-start(bf16[1,1,3,128,128]{4,3,2,1,0:T(8,128)(2,1)} %param.9) | copy-start | bytes 294916
  11.4 0.7 copy-start.5
  12.0 0.7 copy-start.7
  13.5 14.5 %collective-permute-start.2 = (f32[392,128]{1,0:T(8,128)S(1)}, f32[392,128]{1,0:T(8,128)S(1)}, u32[]{:S(2)}, u32[]{:S(2)}) collective-permute-start(f32[392,128]{1,0:T(8,128)S(1)} %get-tuple-element.29), channel_id=1, source_target_pairs={{0,1},{2,3},{1,0},{3,2},{4,5},{6,7},{5,4},{7,6},{8,9},{10,11},{9,8... | collective-permute-start | bytes 602120 | tf_op jit(solution)/shard_map/ppermute | solution.py:378
  15.6 12.4 %collective-permute-start.3 = (f32[392,128]{1,0:T(8,128)S(1)}, f32[392,128]{1,0:T(8,128)S(1)}, u32[]{:S(2)}, u32[]{:S(2)}) collective-permute-start(f32[392,128]{1,0:T(8,128)S(1)} %get-tuple-element.30), channel_id=1, source_target_pairs={{1,2},{2,1},{5,6},{6,5},{9,10},{10,9},{13,14},{14,13},{17,18},{18,... | collective-permute-start | bytes 602120 | tf_op jit(solution)/shard_map/ppermute | solution.py:378
  16.3 15.9 %collective-permute-start = (f32[768,128]{1,0:T(8,128)S(1)}, f32[768,128]{1,0:T(8,128)S(1)}, u32[]{:S(2)}, u32[]{:S(2)}) collective-permute-start(f32[768,128]{1,0:T(8,128)S(1)} %get-tuple-element.26), channel_id=1, source_target_pairs={{0,1},{2,3},{1,0},{3,2},{4,5},{6,7},{5,4},{7,6},{8,9},{10,11},{9,8... | collective-permute-start | bytes 1179656 | tf_op jit(solution)/shard_map/ppermute | solution.py:378
  20.5 11.7 %collective-permute-start.1 = (f32[768,128]{1,0:T(8,128)S(1)}, f32[768,128]{1,0:T(8,128)S(1)}, u32[]{:S(2)}, u32[]{:S(2)}) collective-permute-start(f32[768,128]{1,0:T(8,128)S(1)} %get-tuple-element.27), channel_id=1, source_target_pairs={{1,2},{2,1},{5,6},{6,5},{9,10},{10,9},{13,14},{14,13},{17,18},{18,... | collective-permute-start | bytes 1179656 | tf_op jit(solution)/shard_map/ppermute | solution.py:378
  24.2 1.1 %copy-start.1 = (f32[4,2,192,128]{3,2,1,0:T(8,128)S(1)}, f32[4,2,192,128]{3,2,1,0:T(8,128)}, u32[]{:S(2)}) copy-start(f32[4,2,192,128]{3,2,1,0:T(8,128)} %potential_ref.3) | copy-start | bytes 2359300
  25.4 0.9 %copy-start.4 = (bf16[1,1,3,128,128]{4,3,2,1,0:T(8,128)(2,1)S(1)}, bf16[1,1,3,128,128]{4,3,2,1,0:T(8,128)(2,1)}, u32[]{:S(2)}) copy-start(bf16[1,1,3,128,128]{4,3,2,1,0:T(8,128)(2,1)} %param.9) | copy-start | bytes 294916
  26.3 1.2 %copy-start.9 = (bf16[8,256,256]{2,1,0:T(8,128)(2,1)S(1)}, bf16[8,256,256]{2,1,0:T(8,128)(2,1)}, u32[]{:S(2)}) copy-start(bf16[8,256,256]{2,1,0:T(8,128)(2,1)} %constant.8.clone.tables_ref) | copy-start | bytes 3145732
  38.3 21.7 %all-to-all-start.1 = ((f32[4,136,256]{2,1,0:T(8,128)}), f32[4,136,256]{2,1,0:T(8,128)S(1)}, u32[]{:S(2)}, u32[]{:S(2)}) async-start(f32[4,136,256]{2,1,0:T(8,128)} %get-tuple-element.45), calls=%async_computation.1 | async-start | bytes 1114112 | tf_op jit(solution)/shard_map/all_to_all | solution.py:469
  44.6 24.6 %collective-permute-start.5 = (f32[768,128]{1,0:T(8,128)S(1)}, f32[768,128]{1,0:T(8,128)S(1)}, u32[]{:S(2)}, u32[]{:S(2)}) collective-permute-start(f32[768,128]{1,0:T(8,128)S(1)} %pad_maximum_fusion.1), channel_id=1, source_target_pairs={{1,2},{2,1},{5,6},{6,5},{9,10},{10,9},{13,14},{14,13},{17,18},{18,... | collective-permute-start | bytes 1179656 | tf_op jit(solution)/shard_map/ppermute | solution.py:378
  45.3 23.9 %collective-permute-start.4 = (f32[768,128]{1,0:T(8,128)S(1)}, f32[768,128]{1,0:T(8,128)S(1)}, u32[]{:S(2)}, u32[]{:S(2)}) collective-permute-start(f32[768,128]{1,0:T(8,128)S(1)} %pad_maximum_fusion), channel_id=1, source_target_pairs={{0,1},{2,3},{1,0},{3,2},{4,5},{6,7},{5,4},{7,6},{8,9},{10,11},{9,8... | collective-permute-start | bytes 1179656 | tf_op jit(solution)/shard_map/ppermute | solution.py:378
  60.0 3.9 %collective-permute-start.8 = (f32[8,128]{1,0:T(8,128)S(1)}, f32[8,128]{1,0:T(8,128)S(1)}, u32[]{:S(2)}, u32[]{:S(2)}) collective-permute-start(f32[8,128]{1,0:T(8,128)S(1)} %slice_reduce_fusion), channel_id=1, source_target_pairs={{0,12},{4,8},{8,4},{12,0},{16,28},{20,24},{24,20},{28,16},{1,13},{... | collective-permute-start | bytes 12296 | tf_op jit(solution)/shard_map/ppermute | solution.py:358
  60.0 5.4 %collective-permute-start.7 = (f32[8,128]{1,0:T(8,128)S(1)}, f32[8,128]{1,0:T(8,128)S(1)}, u32[]{:S(2)}, u32[]{:S(2)}) collective-permute-start(f32[8,128]{1,0:T(8,128)S(1)} %slice_reduce_fusion), channel_id=1, source_target_pairs={{0,8},{4,12},{8,0},{12,4},{16,24},{20,28},{24,16},{28,20},{1,9},{5... | collective-permute-start | bytes 12296 | tf_op jit(solution)/shard_map/ppermute | solution.py:358
  63.9 1.6 %collective-permute-start.6 = (f32[8,128]{1,0:T(8,128)S(1)}, f32[8,128]{1,0:T(8,128)S(1)}, u32[]{:S(2)}, u32[]{:S(2)}) collective-permute-start(f32[8,128]{1,0:T(8,128)S(1)} %slice_reduce_fusion), channel_id=1, source_target_pairs={{0,4},{4,0},{8,12},{12,8},{16,20},{20,16},{24,28},{28,24},{1,5},{5... | collective-permute-start | bytes 12296 | tf_op jit(solution)/shard_map/ppermute | solution.py:358
  65.5 3.7 %collective-permute-start.9 = (f32[8,128]{1,0:T(8,128)S(1)}, f32[8,128]{1,0:T(8,128)S(1)}, u32[]{:S(2)}, u32[]{:S(2)}) collective-permute-start(f32[8,128]{1,0:T(8,128)S(1)} %add_add_fusion), channel_id=1, source_target_pairs={{0,16},{4,20},{8,24},{12,28},{16,0},{20,4},{24,8},{28,12},{1,17},{... | collective-permute-start | bytes 12296 | tf_op jit(solution)/shard_map/ppermute | solution.py:358
